TPU v7x, 256 devices: a whole 4x4x8 slice. The times are simulated.
256 devices in a mesh: dp: 256 (over x, y, z, core).
Axes of the slice: x: 4, y: 4, z: 8, core: 2. Of those that a mesh axis runs over, the one named last changes fastest.
Arguments:
- image_feats: bfloat16 [98304, 1152], P('dp'), may hold values from -0.26516504 to 0.26516504
- text_feats: bfloat16 [98304, 1152], P('dp'), may hold values from -0.26516504 to 0.26516504
- log_scale: float32 [], replicated, may hold values from 1.6 to 2.6
- bias: float32 [], replicated, may hold values from -5 to -2
Outputs:
- grad_image: float32 [98304, 1152], P('dp')
- grad_text: float32 [98304, 1152], P('dp')
- stats: float32 [3], replicated
All inputs are finite; a program needn't handle non-finite values.
Results may differ from a plain program's by a relative error of at most 0.00058.
Values may be sent and summed in bfloat16 or wider, within the bound.
No kernel may reach another device: no remote copies, remote signals or barrier semaphores. Data moves between devices by JAX's collectives and lax.ppermute only.
A program may use at most 128 MiB of HBM per device.

v0:
```python
import jax
import jax.numpy as jnp
from jax import lax
from jax.sharding import PartitionSpec as P

STEPS = 8


def passed_along(value, axis, steps):
    count = lax.axis_size(axis)
    pairs = [(source, (source + steps) % count) for source in range(count)]
    return lax.ppermute(value, axis, pairs)


def normalize(raw):
    values = raw.astype(jnp.float32)
    inverse = lax.rsqrt(jnp.sum(values * values, axis=-1, keepdims=True) + 1e-06)
    return (values * inverse, inverse)


def tile_block(image_bf, text_bf, scale, bias, label):
    sim = lax.dot_general(
        image_bf, text_bf, (((1,), (1,)), ((), ())), preferred_element_type=jnp.float32
    )
    logit = scale * sim + bias
    grad = jax.nn.sigmoid(logit) - label
    tile = (scale * grad).astype(jnp.bfloat16)
    return (sim, logit, grad, tile)


def pair_block(image_bf, text_bf, scale, bias, label):
    sim, logit, grad, tile = tile_block(image_bf, text_bf, scale, bias, label)
    sign = 2.0 * label - 1.0
    loss_part = jnp.sum(jax.nn.softplus(-sign * logit))
    scale_part = jnp.sum(grad * sim) * scale
    bias_part = jnp.sum(grad)
    image_term = jnp.dot(tile, text_bf, preferred_element_type=jnp.float32)
    text_term = lax.dot_general(
        tile, image_bf, (((0,), (0,)), ((), ())), preferred_element_type=jnp.float32
    )
    return (image_term, text_term, loss_part, scale_part, bias_part)


def per_device(image_feats, text_feats, log_scale, bias):
    ximg, rimg = normalize(image_feats)
    xtxt, rtxt = normalize(text_feats)
    image_bf = ximg.astype(jnp.bfloat16)
    text_bf = xtxt.astype(jnp.bfloat16)
    scale = jnp.exp(log_scale)
    rows = image_bf.shape[0]
    positions = lax.broadcasted_iota(jnp.int32, (rows, rows), 0)
    columns = lax.broadcasted_iota(jnp.int32, (rows, rows), 1)
    diagonal = (positions == columns).astype(jnp.float32)
    no_label = jnp.zeros_like(diagonal)
    grad_x = jnp.zeros(ximg.shape, jnp.float32)
    loss_sum = jnp.float32(0.0)
    scale_sum = jnp.float32(0.0)
    bias_sum = jnp.float32(0.0)
    visiting = text_bf
    partial_sum = jnp.zeros(xtxt.shape, jnp.float32)
    for step in range(STEPS):
        if step > 0:
            visiting = passed_along(visiting, "dp", 1)
            partial_sum = passed_along(partial_sum, "dp", 1)
        label = diagonal if step == 0 else no_label
        image_term, text_term, loss_part, scale_part, bias_part = pair_block(
            image_bf, visiting, scale, bias, label
        )
        grad_x = grad_x + image_term
        partial_sum = partial_sum + text_term
        loss_sum = loss_sum + loss_part
        scale_sum = scale_sum + scale_part
        bias_sum = bias_sum + bias_part
    grad_y = passed_along(partial_sum, "dp", -(STEPS - 1))
    loss_all, scale_all, bias_all = lax.psum((loss_sum, scale_sum, bias_sum), "dp")
    grad_image = rimg * (grad_x - ximg * jnp.sum(ximg * grad_x, axis=-1, keepdims=True))
    grad_text = rtxt * (grad_y - xtxt * jnp.sum(xtxt * grad_y, axis=-1, keepdims=True))
    divisor = jnp.float32(rows * lax.axis_size("dp") * STEPS)
    stats = jnp.stack([loss_all, scale_all, bias_all]) / divisor
    return (grad_image, grad_text, stats)


def solution(mesh):
    in_specs = (P("dp", None), P("dp", None), P(), P())
    out_specs = (P("dp", None), P("dp", None), P())
    return jax.shard_map(
        per_device, mesh=mesh, in_specs=in_specs, out_specs=out_specs, check_vma=False
    )
```

profile of v0, /device:TPU:16, one launch (start us, length us, event | category | flops | bytes accessed | tf_op | source)
XLA Modules:
  0.0 443.6 jit_solution(17749266098243933452)
XLA Ops:
  5.2 1.8 fusion.14
  7.9 2.0 collective-permute-start
  10.0 32.8 %collective-permute-done = bf16[384,1152]{1,0:T(8,128)(2,1)S(1)} collective-permute-done((bf16[384,1152]{1,0:T(8,128)(2,1)S(1)}, bf16[384,1152]{1,0:T(8,128)(2,1)S(1)}, u32[]{:S(2)}, u32[]{:S(2)}) %collective-permute-start) | collective-permute-done | bytes 884768 | tf_op jit(solution)/shard_map/ppermute | solution.py:12
  42.8 1.8 fusion.15
  45.6 33.4 %collective-permute-done.1 = bf16[384,1152]{1,0:T(8,128)(2,1)S(1)} collective-permute-done((bf16[384,1152]{1,0:T(8,128)(2,1)S(1)}, bf16[384,1152]{1,0:T(8,128)(2,1)S(1)}, u32[]{:S(2)}, u32[]{:S(2)}) %collective-permute-start.1) | collective-permute-done | bytes 884768 | tf_op jit(solution)/shard_map/ppermute | solution.py:12
  79.0 1.8 fusion.16
  82.3 33.2 %collective-permute-done.2 = bf16[384,1152]{1,0:T(8,128)(2,1)S(1)} collective-permute-done((bf16[384,1152]{1,0:T(8,128)(2,1)S(1)}, bf16[384,1152]{1,0:T(8,128)(2,1)S(1)}, u32[]{:S(2)}, u32[]{:S(2)}) %collective-permute-start.2) | collective-permute-done | bytes 884768 | tf_op jit(solution)/shard_map/ppermute | solution.py:12
  118.5 33.4 %collective-permute-done.3 = bf16[384,1152]{1,0:T(8,128)(2,1)S(1)} collective-permute-done((bf16[384,1152]{1,0:T(8,128)(2,1)S(1)}, bf16[384,1152]{1,0:T(8,128)(2,1)S(1)}, u32[]{:S(2)}, u32[]{:S(2)}) %collective-permute-start.3) | collective-permute-done | bytes 884768 | tf_op jit(solution)/shard_map/ppermute | solution.py:12
  151.9 1.7 fusion.18
  154.9 33.4 %collective-permute-done.4 = bf16[384,1152]{1,0:T(8,128)(2,1)S(1)} collective-permute-done((bf16[384,1152]{1,0:T(8,128)(2,1)S(1)}, bf16[384,1152]{1,0:T(8,128)(2,1)S(1)}, u32[]{:S(2)}, u32[]{:S(2)}) %collective-permute-start.4) | collective-permute-done | bytes 884768 | tf_op jit(solution)/shard_map/ppermute | solution.py:12
  188.3 1.8 fusion.19
  192.2 32.5 %collective-permute-done.5 = bf16[384,1152]{1,0:T(8,128)(2,1)S(1)} collective-permute-done((bf16[384,1152]{1,0:T(8,128)(2,1)S(1)}, bf16[384,1152]{1,0:T(8,128)(2,1)S(1)}, u32[]{:S(2)}, u32[]{:S(2)}) %collective-permute-start.5) | collective-permute-done | bytes 884768 | tf_op jit(solution)/shard_map/ppermute | solution.py:12
  224.8 1.8 fusion.20
  235.2 3.2 convolution_add_fusion.6
  240.2 2.6 convolution_add_fusion.5
  244.6 3.2 convolution_add_fusion.4
  249.8 33.0 %collective-permute-done.6 = bf16[384,1152]{1,0:T(8,128)(2,1)} collective-permute-done((bf16[384,1152]{1,0:T(8,128)(2,1)}, bf16[384,1152]{1,0:T(8,128)(2,1)}, u32[]{:S(2)}, u32[]{:S(2)}) %collective-permute-start.6) | collective-permute-done | bytes 884768 | tf_op jit(solution)/shard_map/ppermute | solution.py:12
  282.8 2.9 fusion.21
  286.6 3.1 add.243
  289.7 1.9 convolution_add_fusion.3
  293.4 3.8 convolution_add_fusion.2
  299.1 135.8 %all-reduce = (f32[1]{0:T(128)}, f32[1]{0:T(128)}, f32[1]{0:T(128)}) all-reduce(f32[1]{0:T(128)} %bitcast.2, f32[1]{0:T(128)} %bitcast.1, f32[1]{0:T(128)} %bitcast), channel_id=1, replica_groups=mesh['dp'=256] {'dp'}, use_global_device_ids=true, to_apply=%region_30.31 | all-reduce | flops 3 | bytes 24 | tf_op jit(solution)/shard_map/psum | solution.py:75
  435.0 2.4 maximum_multiply_fusion
  437.4 2.7 fusion.6
  (78 shorter events, 20.1 us)
Async XLA Ops:
  0.6 4.6 %copy-start.2 = (bf16[384,1152]{1,0:T(8,128)(2,1)S(1)}, bf16[384,1152]{1,0:T(8,128)(2,1)}, u32[]{:S(2)}) copy-start(bf16[384,1152]{1,0:T(8,128)(2,1)} %param.4) | copy-start | bytes 2654212
  0.6 3.0 copy-start
  7.8 36.7 %collective-permute-start.7 = (f32[384,1152]{1,0:T(8,128)S(1)}, f32[384,1152]{1,0:T(8,128)S(1)}, u32[]{:S(2)}, u32[]{:S(2)}) collective-permute-start(f32[384,1152]{1,0:T(8,128)S(1)} %fusion.22), channel_id=1, source_target_pairs={{0,1},{1,2},{2,3},{3,4},{4,5},{5,6},{6,7},{7,8},{8,9},{9,10},{10,1... | collective-permute-start | bytes 5308424 | tf_op jit(solution)/shard_map/ppermute | solution.py:12
  7.9 34.9 %collective-permute-start = (bf16[384,1152]{1,0:T(8,128)(2,1)S(1)}, bf16[384,1152]{1,0:T(8,128)(2,1)S(1)}, u32[]{:S(2)}, u32[]{:S(2)}) collective-permute-start(bf16[384,1152]{1,0:T(8,128)(2,1)S(1)} %fusion.2), channel_id=1, source_target_pairs={{0,1},{1,2},{2,3},{3,4},{4,5},{5,6},{6,7},{7,8},{8,9},{9,10},{10,1... | collective-permute-start | bytes 2654216 | tf_op jit(solution)/shard_map/ppermute | solution.py:12
  45.4 36.3 %collective-permute-start.8 = (f32[384,1152]{1,0:T(8,128)S(1)}, f32[384,1152]{1,0:T(8,128)S(1)}, u32[]{:S(2)}, u32[]{:S(2)}) collective-permute-start(f32[384,1152]{1,0:T(8,128)S(1)} %convolution_add_fusion), channel_id=1, source_target_pairs={{0,1},{1,2},{2,3},{3,4},{4,5},{5,6},{6,7},{7,8},{8,9},{9,10},{10,1... | collective-permute-start | bytes 5308424 | tf_op jit(solution)/shard_map/ppermute | solution.py:12
  45.5 33.5 %collective-permute-start.1 = (bf16[384,1152]{1,0:T(8,128)(2,1)S(1)}, bf16[384,1152]{1,0:T(8,128)(2,1)S(1)}, u32[]{:S(2)}, u32[]{:S(2)}) collective-permute-start(bf16[384,1152]{1,0:T(8,128)(2,1)S(1)} %collective-permute-done), channel_id=1, source_target_pairs={{0,1},{1,2},{2,3},{3,4},{4,5},{5,6},{6,7},{7,8},{8,9},{9,10},{10,1... | collective-permute-start | bytes 2654216 | tf_op jit(solution)/shard_map/ppermute | solution.py:12
  79.0 2.9 copy-start.3
  81.9 36.2 %collective-permute-start.9 = (f32[384,1152]{1,0:T(8,128)S(1)}, f32[384,1152]{1,0:T(8,128)S(1)}, u32[]{:S(2)}, u32[]{:S(2)}) collective-permute-start(f32[384,1152]{1,0:T(8,128)S(1)} %add.238), channel_id=1, source_target_pairs={{0,1},{1,2},{2,3},{3,4},{4,5},{5,6},{6,7},{7,8},{8,9},{9,10},{10,1... | collective-permute-start | bytes 5308424 | tf_op jit(solution)/shard_map/ppermute | solution.py:12
  82.0 33.5 %collective-permute-start.2 = (bf16[384,1152]{1,0:T(8,128)(2,1)S(1)}, bf16[384,1152]{1,0:T(8,128)(2,1)S(1)}, u32[]{:S(2)}, u32[]{:S(2)}) collective-permute-start(bf16[384,1152]{1,0:T(8,128)(2,1)S(1)} %collective-permute-done.1), channel_id=1, source_target_pairs={{0,1},{1,2},{2,3},{3,4},{4,5},{5,6},{6,7},{7,8},{8,9},{9,10},{10,1... | collective-permute-start | bytes 2654216 | tf_op jit(solution)/shard_map/ppermute | solution.py:12
  115.5 2.9 copy-start.4
  118.3 36.2 %collective-permute-start.10 = (f32[384,1152]{1,0:T(8,128)S(1)}, f32[384,1152]{1,0:T(8,128)S(1)}, u32[]{:S(2)}, u32[]{:S(2)}) collective-permute-start(f32[384,1152]{1,0:T(8,128)S(1)} %add.239), channel_id=1, source_target_pairs={{0,1},{1,2},{2,3},{3,4},{4,5},{5,6},{6,7},{7,8},{8,9},{9,10},{10,1... | collective-permute-start | bytes 5308424 | tf_op jit(solution)/shard_map/ppermute | solution.py:12
  118.4 33.5 %collective-permute-start.3 = (bf16[384,1152]{1,0:T(8,128)(2,1)S(1)}, bf16[384,1152]{1,0:T(8,128)(2,1)S(1)}, u32[]{:S(2)}, u32[]{:S(2)}) collective-permute-start(bf16[384,1152]{1,0:T(8,128)(2,1)S(1)} %collective-permute-done.2), channel_id=1, source_target_pairs={{0,1},{1,2},{2,3},{3,4},{4,5},{5,6},{6,7},{7,8},{8,9},{9,10},{10,1... | collective-permute-start | bytes 2654216 | tf_op jit(solution)/shard_map/ppermute | solution.py:12
  151.9 2.9 copy-start.7
  154.7 36.3 %collective-permute-start.11 = (f32[384,1152]{1,0:T(8,128)S(1)}, f32[384,1152]{1,0:T(8,128)S(1)}, u32[]{:S(2)}, u32[]{:S(2)}) collective-permute-start(f32[384,1152]{1,0:T(8,128)S(1)} %add.240), channel_id=1, source_target_pairs={{0,1},{1,2},{2,3},{3,4},{4,5},{5,6},{6,7},{7,8},{8,9},{9,10},{10,1... | collective-permute-start | bytes 5308424 | tf_op jit(solution)/shard_map/ppermute | solution.py:12
  154.8 33.5 %collective-permute-start.4 = (bf16[384,1152]{1,0:T(8,128)(2,1)S(1)}, bf16[384,1152]{1,0:T(8,128)(2,1)S(1)}, u32[]{:S(2)}, u32[]{:S(2)}) collective-permute-start(bf16[384,1152]{1,0:T(8,128)(2,1)S(1)} %collective-permute-done.3), channel_id=1, source_target_pairs={{0,1},{1,2},{2,3},{3,4},{4,5},{5,6},{6,7},{7,8},{8,9},{9,10},{10,1... | collective-permute-start | bytes 2654216 | tf_op jit(solution)/shard_map/ppermute | solution.py:12
  188.3 2.9 copy-start.5
  191.2 36.2 %collective-permute-start.12 = (f32[384,1152]{1,0:T(8,128)S(1)}, f32[384,1152]{1,0:T(8,128)S(1)}, u32[]{:S(2)}, u32[]{:S(2)}) collective-permute-start(f32[384,1152]{1,0:T(8,128)S(1)} %add.241), channel_id=1, source_target_pairs={{0,1},{1,2},{2,3},{3,4},{4,5},{5,6},{6,7},{7,8},{8,9},{9,10},{10,1... | collective-permute-start | bytes 5308424 | tf_op jit(solution)/shard_map/ppermute | solution.py:12
  191.3 33.5 %collective-permute-start.5 = (bf16[384,1152]{1,0:T(8,128)(2,1)S(1)}, bf16[384,1152]{1,0:T(8,128)(2,1)S(1)}, u32[]{:S(2)}, u32[]{:S(2)}) collective-permute-start(bf16[384,1152]{1,0:T(8,128)(2,1)S(1)} %collective-permute-done.4), channel_id=1, source_target_pairs={{0,1},{1,2},{2,3},{3,4},{4,5},{5,6},{6,7},{7,8},{8,9},{9,10},{10,1... | collective-permute-start | bytes 2654216 | tf_op jit(solution)/shard_map/ppermute | solution.py:12
  228.8 57.8 %collective-permute-start.13 = (f32[384,1152]{1,0:T(8,128)}, f32[384,1152]{1,0:T(8,128)}, u32[]{:S(2)}, u32[]{:S(2)}) collective-permute-start(f32[384,1152]{1,0:T(8,128)} %add.242), channel_id=1, source_target_pairs={{0,1},{1,2},{2,3},{3,4},{4,5},{5,6},{6,7},{7,8},{8,9},{9,10},{10,1... | collective-permute-start | bytes 5308424 | tf_op jit(solution)/shard_map/ppermute | solution.py:12
  235.1 47.7 %collective-permute-start.6 = (bf16[384,1152]{1,0:T(8,128)(2,1)}, bf16[384,1152]{1,0:T(8,128)(2,1)}, u32[]{:S(2)}, u32[]{:S(2)}) collective-permute-start(bf16[384,1152]{1,0:T(8,128)(2,1)} %copy-done.8), channel_id=1, source_target_pairs={{0,1},{1,2},{2,3},{3,4},{4,5},{5,6},{6,7},{7,8},{8,9},{9,10},{10,1... | collective-permute-start | bytes 2654216 | tf_op jit(solution)/shard_map/ppermute | solution.py:12
  286.6 3.1 copy-start.1
  286.6 3.1 copy-start.6
  286.6 3.1 copy-start.12
  289.7 152.0 %collective-permute-start.14 = (f32[384,1152]{1,0:T(8,128)}, f32[384,1152]{1,0:T(8,128)S(1)}, u32[]{:S(2)}, u32[]{:S(2)}) collective-permute-start(f32[384,1152]{1,0:T(8,128)} %add.243), channel_id=1, source_target_pairs={{0,249},{1,250},{2,251},{3,252},{4,253},{5,254},{6,255},{7,0},{8,1... | collective-permute-start | bytes 5308424 | tf_op jit(solution)/shard_map/ppermute | solution.py:12
  (7 other events, 6.9 us)
where the time goes:
time: 447 us; the launch traced here: 444 us
  waiting for transfers between devices  232 us (52%)
  blocking collectives  136 us (30%)
  matrix products  40.6 us (9%)
  between operations  17.4 us (4%)
  other arithmetic  14.3 us (3%)
    ppermute x15, waiting for transfers between devices, passed_along(): return lax.ppermute(value, axis, pairs)  232 us
    psum x1, blocking collectives, per_device(): lax.psum((loss_sum, scale_sum, bias_sum), 'dp')  136 us
    dot_general x8, matrix products, pair_block(): image_term = jnp.dot(tile, text_bf, preferred_element_type=jnp.float32)  18.7 us
    dot_general x8, matrix products, tile_block(): lax.dot_general(image_bf, text_bf, (((1,), (1,)), ((), ())), preferred_el...  15.2 us
  transfers between devices with their start and end apart: 15, of which 7 were waited for; matrix products, arithmetic and copies ran while one was open for 9% of the time, Pallas kernels for 0%

commit v1 on v0

v1 whole, which is shorter than its diff:
```python
import functools

import jax
import jax.numpy as jnp
from jax import lax
from jax.experimental import pallas as pl
from jax.experimental.pallas import tpu as pltpu
from jax.sharding import PartitionSpec as P

STEPS = 8
EPS = 1e-06
LOG2_E = 1.4426950408889634
LN_2 = 0.6931471805599453
ROUNDS = (1, 16, 32, 64, 128, 2, 4, 8)
VMEM_LIMIT = 24 * 1024 * 1024
SMEM = pl.BlockSpec(memory_space=pltpu.SMEM)
VMEM = pl.BlockSpec(memory_space=pltpu.VMEM)
HBM = pl.BlockSpec(memory_space=pltpu.HBM)


def my_core():
    return lax.rem(lax.axis_index("dp"), 2)


def inverse_norm(values):
    return lax.rsqrt(jnp.sum(values * values, axis=-1, keepdims=True) + EPS)


def fetch_own(x_ref, y_ref, raw, sems, want_image):
    pieces = sems.shape[0]
    size = raw.shape[0] // pieces
    for i in range(pieces):
        part = pl.ds(i * size, size)

        @pl.when(want_image)
        def _():
            pltpu.make_async_copy(x_ref.at[part], raw.at[part], sems.at[i]).start()

        @pl.when(jnp.logical_not(want_image))
        def _():
            pltpu.make_async_copy(y_ref.at[part], raw.at[part], sems.at[i]).start()


def normalize_kernel(x_ref, y_ref, a_ref, b_ref, raw, sems):
    core = my_core()
    sides = ((a_ref, core == 0), (b_ref, core == 1))
    for side, (_, want_image) in enumerate(sides):
        fetch_own(x_ref, y_ref, raw.at[side], sems.at[side], want_image)
    pieces = sems.shape[1]
    size = raw.shape[1] // pieces
    for side, (out_ref, _) in enumerate(sides):
        for i in range(pieces):
            part = pl.ds(i * size, size)
            pltpu.make_async_copy(x_ref.at[part], raw.at[side, part], sems.at[side, i]).wait()
            for start in range(i * size, (i + 1) * size, 48):
                block = slice(start, start + 48)
                values = raw[side, block, :].astype(jnp.float32)
                out_ref[block, :] = (values * inverse_norm(values)).astype(jnp.bfloat16)


def normalized(x, y):
    return pl.pallas_call(
        normalize_kernel,
        out_shape=[jax.ShapeDtypeStruct(x.shape, jnp.bfloat16)] * 2,
        in_specs=[HBM, HBM],
        out_specs=[VMEM, VMEM],
        scratch_shapes=[pltpu.VMEM((2, *x.shape), jnp.bfloat16), pltpu.SemaphoreType.DMA((2, 2))],
        compiler_params=pltpu.CompilerParams(vmem_limit_bytes=VMEM_LIMIT),
        cost_estimate=pl.CostEstimate(
            flops=4 * x.size, bytes_accessed=8 * x.size, transcendentals=0
        ),
    )(x, y)


def folded(values):
    rows, columns = values.shape
    total = jnp.sum(values.reshape(rows // 8, 8, columns), axis=0)
    out = total[:, :128]
    for start in range(128, columns, 128):
        out = out + total[:, start : start + 128]
    return out


def negatives(sim, scalars, stats, weight):
    power = jnp.exp2(sim * scalars[2] + scalars[3])
    above = 1.0 + power
    inverse = pl.reciprocal(above, approx=True)
    inverse = inverse * (2.0 - above * inverse)
    grad = power * inverse
    if stats is not None:
        rest = (power - (above - 1.0)) * inverse
        parts = (folded(jnp.log2(above)), folded(rest), folded(grad * sim), folded(grad))
        for row, part in enumerate(parts):
            stats[row * 8 : row * 8 + 8, :] += part if weight is None else part * weight
    return scalars[0] * grad


def cut(blocks, width):
    pieces, current, room = [], [], width
    for index, rows in enumerate(blocks):
        start = 0
        while start < rows:
            take = min(room, rows - start)
            current.append((index, start, take))
            start, room = start + take, room - take
            if room == 0:
                pieces.append(current)
                current, room = [], width
    if current:
        pieces.append(current)
    return pieces


def joined(blocks, piece=None):
    if piece is None:
        piece = [(i, 0, block.shape[0]) for i, block in enumerate(blocks)]
    values = [blocks[i][start : start + take, :] for i, start, take in piece]
    return values[0] if len(values) == 1 else jnp.concatenate(values, axis=0)


def stage_kernel(plan, *refs):
    modes, label, has_acc, image_core, has_outs = plan
    refs = list(refs)
    scalars, own = refs.pop(0), refs.pop(0)
    blocks = [refs.pop(0) for _ in modes]
    acc_in = refs.pop(0) if has_acc else None
    if image_core is not None:
        x_ref, y_ref = refs.pop(0), refs.pop(0)
        if has_outs:
            refs = refs[2:]
        out_image, out_text = refs.pop(0), refs.pop(0)
    else:
        acc = refs.pop(0)
    stats = refs.pop(0) if any(m is not None for m in modes) else None
    tiles = refs.pop(0)
    core = my_core()
    if image_core is not None:
        acc, raw, sems, out_sems = refs
        is_image = core == image_core
        fetch_own(x_ref, y_ref, raw, sems, is_image)
    if stats is not None:
        stats[...] = jnp.zeros_like(stats)
    weight = core.astype(jnp.float32)
    weights = {"all": None, "core1": weight, "core0": 1.0 - weight}
    rows = own.shape[0]
    column = 0
    for piece in cut([block.shape[0] for block in blocks], 256):
        other = joined(blocks, piece)
        sim = lax.dot_general(
            own[...], other, (((1,), (1,)), ((), ())), preferred_element_type=jnp.float32
        )
        offset = 0
        for i, start, take in piece:
            part = sim[:, offset : offset + take]
            mode = modes[i]
            grad = negatives(part, scalars, None if mode is None else stats, weights.get(mode))
            if label and i == 0:
                across = lax.broadcasted_iota(jnp.int32, part.shape, 0)
                along = lax.broadcasted_iota(jnp.int32, part.shape, 1) + start
                positive = across == along
                if mode is not None:
                    zero = jnp.zeros_like(part)
                    logit = scalars[0] * part + scalars[1]
                    stats[8:16, :] -= folded(jnp.where(positive, logit, zero))
                    stats[16:24, :] -= folded(jnp.where(positive, part, zero))
                    stats[24:32, :] -= folded(positive.astype(jnp.float32))
                grad = jnp.where(positive, grad - scalars[0], grad)
            tiles[:, column : column + take] = grad.astype(jnp.bfloat16)
            offset, column = offset + take, column + take
    term = jnp.dot(tiles[...], joined(blocks), preferred_element_type=jnp.float32)
    acc[...] = term if acc_in is None else acc_in[...] + term
    if image_core is None:
        return
    pieces = sems.shape[0]
    size = rows // pieces
    for i in range(pieces):
        part = pl.ds(i * size, size)
        pltpu.make_async_copy(x_ref.at[part], raw.at[part], sems.at[i]).wait()
        for start in range(i * size, (i + 1) * size, 48):
            block = slice(start, start + 48)
            values = raw[block, :].astype(jnp.float32)
            inverse = inverse_norm(values)
            unit = values * inverse
            total = acc[block, :]
            acc[block, :] = inverse * (
                total - unit * jnp.sum(unit * total, axis=-1, keepdims=True)
            )

        @pl.when(is_image)
        def _():
            pltpu.make_async_copy(acc.at[part], out_image.at[part], out_sems.at[i]).start()

        @pl.when(jnp.logical_not(is_image))
        def _():
            pltpu.make_async_copy(acc.at[part], out_text.at[part], out_sems.at[i]).start()

    for i in range(pieces):
        part = pl.ds(i * size, size)
        pltpu.make_async_copy(acc.at[part], out_image.at[part], out_sems.at[i]).wait()


def middle_kernel(plan, *refs):
    scalars, stats = refs[0], refs[-1]
    blocks = refs[1:-1]
    odd = my_core() == 1
    stats[...] = jnp.zeros_like(stats)

    def chosen(pair):
        views = [blocks[i][start : start + size, :] for i, start, size in pair]
        return views[0] if len(views) == 1 else jnp.where(odd, views[0], views[1])

    for left, right in plan:
        one, other = chosen(left), chosen(right)
        for start in range(0, other.shape[0], 256):
            sim = lax.dot_general(
                one, other[start : start + 256], (((1,), (1,)), ((), ())),
                preferred_element_type=jnp.float32,
            )
            negatives(sim, scalars, stats, None)


def middle(scalars, blocks, plan):
    rows, width = blocks[0].shape
    pairs = sum(left[0][2] * right[0][2] for left, right in plan)
    return pl.pallas_call(
        functools.partial(middle_kernel, plan),
        out_shape=jax.ShapeDtypeStruct((32, 128), jnp.float32),
        in_specs=[SMEM] + [VMEM] * len(blocks),
        out_specs=VMEM,
        compiler_params=pltpu.CompilerParams(vmem_limit_bytes=VMEM_LIMIT),
        cost_estimate=pl.CostEstimate(
            flops=2 * pairs * width, bytes_accessed=2 * rows * width, transcendentals=3 * pairs
        ),
    )(scalars, *blocks)


def stage(scalars, own, blocks, modes, acc=None, label=False, final=None):
    rows, width = own.shape
    big = jax.ShapeDtypeStruct((rows, width), jnp.float32)
    args, in_specs = [scalars, own, *blocks], [SMEM, VMEM] + [VMEM] * len(blocks)
    scratch = [pltpu.VMEM((rows, sum(block.shape[0] for block in blocks)), jnp.bfloat16)]
    aliases, image_core, has_outs = {}, None, False
    if acc is not None:
        args.append(acc)
        in_specs.append(VMEM)
    if final is None:
        if acc is not None:
            aliases = {len(args) - 1: 0}
        out_shape, out_specs = [big], [VMEM]
    else:
        image_core, x, y, outs = final
        args += [x, y]
        in_specs += [HBM, HBM]
        if outs is not None:
            has_outs = True
            aliases = {len(args): 0, len(args) + 1: 1}
            args += list(outs)
            in_specs += [HBM, HBM]
        out_shape, out_specs = [big, big], [HBM, HBM]
        scratch += [
            pltpu.VMEM((rows, width), jnp.float32),
            pltpu.VMEM((rows, width), jnp.bfloat16),
            pltpu.SemaphoreType.DMA((4,)),
            pltpu.SemaphoreType.DMA((4,)),
        ]
    if any(m is not None for m in modes):
        out_shape.append(jax.ShapeDtypeStruct((32, 128), jnp.float32))
        out_specs.append(VMEM)
    plan = (tuple(modes), label, acc is not None, image_core, has_outs)
    pairs = rows * sum(block.shape[0] for block in blocks)
    return pl.pallas_call(
        functools.partial(stage_kernel, plan),
        out_shape=out_shape,
        in_specs=in_specs,
        out_specs=out_specs,
        scratch_shapes=scratch,
        input_output_aliases=aliases,
        compiler_params=pltpu.CompilerParams(vmem_limit_bytes=VMEM_LIMIT),
        cost_estimate=pl.CostEstimate(
            flops=4 * pairs * width, bytes_accessed=10 * rows * width, transcendentals=3 * pairs
        ),
    )(*args)


def finish_kernel(divisor, scalars, stats, out_ref):
    sums = [jnp.sum(stats[row : row + 8, :]) for row in range(0, 32, 8)]
    out_ref[0] = (sums[0] * LN_2 + sums[1]) / divisor
    out_ref[1] = sums[2] * scalars[0] / divisor
    out_ref[2] = sums[3] / divisor


def finished(scalars, stats, divisor):
    return pl.pallas_call(
        functools.partial(finish_kernel, divisor),
        out_shape=jax.ShapeDtypeStruct((3,), jnp.float32),
        in_specs=[SMEM, VMEM],
        out_specs=SMEM,
    )(scalars, stats)


def tied(*values):
    return lax.optimization_barrier(values)


def per_device(image_feats, text_feats, log_scale, bias):
    count = lax.axis_size("dp")
    up_down = [(d, (d + 2 if d % 2 else d - 2) % count) for d in range(count)]
    down_up = [(d, (d - 2 if d % 2 else d + 2) % count) for d in range(count)]
    cross = [(d, (d + 1 if d % 2 else d - 1) % count) for d in range(count)]
    other_core = [(d, d ^ 1) for d in range(count)]
    scale = jnp.exp(log_scale)
    scalars = jnp.stack([scale, bias, scale * LOG2_E, bias * LOG2_E])
    x = pltpu.with_memory_space_constraint(image_feats, pltpu.HBM)
    y = pltpu.with_memory_space_constraint(text_feats, pltpu.HBM)
    rows = image_feats.shape[0]
    half = rows // 2

    def up(value):
        return lax.ppermute(value, "dp", up_down)

    def down(value):
        return lax.ppermute(value, "dp", down_up)

    def swap(value):
        return lax.ppermute(value, "dp", other_core)

    def all_added(value, rounds):
        for distance in rounds:
            if distance < count:
                pairs = [(d, d ^ distance) for d in range(count)]
                value = value + lax.ppermute(value, "dp", pairs)
        return value

    whole = lambda i: (i, 0, rows)
    a, b = normalized(x, y)
    p1 = up(a)
    r1 = down(b)
    sibling = swap(b)
    acc_a, stats0 = stage(scalars, a, [b], ["all"], label=True)

    p1, acc_a = tied(p1, acc_a)
    p2, from_p1 = up(p1), swap(p1)
    acc_b, stats1 = stage(scalars, b, [a, sibling], [None, "core1"], label=True)

    r1, from_p1, acc_b = tied(r1, from_p1, acc_b)
    r2, from_r1 = down(r1), swap(r1)
    acc_a, stats2 = stage(scalars, a, [from_p1, r1], ["core0", None], acc_a)
    stats3 = middle(scalars, [p1, r1], (((whole(0),), (whole(1),)),))

    p2, from_r1, acc_a, stats3 = tied(p2, from_r1, acc_a, stats3)
    p3, from_p2 = up(p2), swap(p2)
    acc_b, stats4 = stage(scalars, b, [p1, from_r1], ["all", "core1"], acc_b)
    stats5 = middle(
        scalars, [p1, r1, from_p1, from_r1, p2],
        (
            ((whole(0), whole(1)), (whole(2), whole(3))),
            ((whole(4),), (whole(1),)),
        ),
    )

    r2, from_p2, acc_b, stats5 = tied(r2, from_p2, acc_b, stats5)
    r3, from_r2 = down(r2), swap(r2)
    stats6 = middle(
        scalars, [p2, r2, from_p1, from_r1, from_p2],
        (
            ((whole(0), whole(1)), (whole(2), whole(3))),
            (((0, 0, half), (4, half, half)), (whole(4), whole(0))),
        ),
    )
    stats = stats0 + stats1 + stats2 + stats3 + stats4 + stats5 + stats6
    stats = all_added(stats, ROUNDS[:1])
    (acc_a,) = stage(scalars, a, [from_p2, r2], [None, None], acc_a)

    p3, from_r2, acc_a, stats = tied(p3, from_r2, acc_a, stats)
    last, from_p3 = lax.ppermute(p3, "dp", cross), swap(p3)
    stats = all_added(stats, ROUNDS[1:3])
    (acc_b,) = stage(scalars, b, [p2, from_r2], [None, None], acc_b)

    r3, from_p3, acc_b, stats = tied(r3, from_p3, acc_b, stats)
    from_r3 = [swap(r3[:half]), swap(r3[half:])]
    stats = all_added(stats, ROUNDS[3:5])
    (acc_a,) = stage(scalars, a, [from_p3, r3], [None, None], acc_a)

    from_r3, acc_a, stats = tied(from_r3, acc_a, stats)
    outs = stage(
        scalars, b, [p3, *from_r3], [None, None, None], acc_b,
        final=(1, x, y, None),
    )
    stats = all_added(stats, ROUNDS[5:])
    sums = finished(scalars, stats, float(rows * count * STEPS))
    last, sums = tied(last, sums)
    grad_image, grad_text = stage(
        scalars, a, [last], [None], acc_a, final=(0, x, y, outs)
    )
    return grad_image, grad_text, sums


def solution(mesh):
    in_specs = (P("dp", None), P("dp", None), P(), P())
    out_specs = (P("dp", None), P("dp", None), P())
    return jax.shard_map(
        per_device, mesh=mesh, in_specs=in_specs, out_specs=out_specs, check_vma=False
    )
```

time: 447 us -> 127 us (0.28)
  waiting for transfers between devices: 232 us -> 47.5 us
  blocking collectives: 136 us -> 0 us
  Pallas kernels: 0 us -> 42.7 us
  matrix products: 40.6 us -> 0 us
  starting transfers between devices: 3.42 us -> 32.7 us
  between operations: 17.4 us -> 2.43 us
  other arithmetic: 14.3 us -> 0.72 us
    ppermute x15 -> x23, waiting for transfers between devices: 232 us -> 47.5 us  [the longest x8 23.9 us: all_added(): value = value + lax.ppermute(value, 'dp', pairs)]
    psum x1 -> x0, blocking collectives: 136 us -> none  [per_device(): lax.psum((loss_sum, scale_sum, bias_sum), 'dp')]
    pallas_call x0 -> x14, Pallas kernels: none -> 42.7 us  [the longest x9 32.1 us: stage(): pl.pallas_call(functools.partial(stage_kernel, plan), out_shape=out_shape...]
    dot_general x24 -> x0, matrix products: 40.6 us -> none  [the longest x8 18.7 us: pair_block(): image_term = jnp.dot(tile, text_bf, preferred_element_type=jnp.float32)]
    ppermute x15 -> x23, starting transfers between devices: 3.42 us -> 32.7 us  [the longest x3 15 us: up(): return lax.ppermute(value, 'dp', up_down)]
    add x6 -> x9, other arithmetic: 5.16 us -> 0.65 us  [the longest x8 0.63 us: all_added(): value = value + lax.ppermute(value, 'dp', pairs)]
  transfers between devices with their start and end apart: 15 -> 23, of which waited for: 7 -> 10; matrix products, arithmetic and copies ran while one was open for 9% -> 1% of each run, Pallas kernels for 0% -> 29%
where the time goes in v1:
time: 127 us
  waiting for transfers between devices  47.5 us (37%)
  Pallas kernels  42.7 us (34%)
  starting transfers between devices  32.7 us (26%)
  between operations  2.43 us (2%)
    pallas_call x9, Pallas kernels, stage(): pl.pallas_call(functools.partial(stage_kernel, plan), out_shape=out_shape...  32.1 us
    ppermute x8, waiting for transfers between devices, all_added(): value = value + lax.ppermute(value, 'dp', pairs)  23.9 us
    ppermute x3, waiting for transfers between devices, up(): return lax.ppermute(value, 'dp', up_down)  23.6 us
    ppermute x3, starting transfers between devices, up(): return lax.ppermute(value, 'dp', up_down)  15 us
    ppermute x8, starting transfers between devices, all_added(): value = value + lax.ppermute(value, 'dp', pairs)  13.3 us
    pallas_call x3, Pallas kernels, middle(): pl.pallas_call(functools.partial(middle_kernel, plan), out_shape=jax.Shap...  7.51 us
    ppermute x1, starting transfers between devices, per_device(): last, from_p3 = (lax.ppermute(p3, 'dp', cross), swap(p3))  3.39 us
  transfers between devices with their start and end apart: 23, of which 10 were waited for; matrix products, arithmetic and copies ran while one was open for 1% of the time, Pallas kernels for 29%

profile of v1, /device:TPU:16, one launch (start us, length us, event | category | flops | bytes accessed | tf_op | source)
XLA Modules:
  0.0 126.7 jit_solution(7635702054640799187)
XLA Ops:
  2.4 5.8 %collective-permute-start = (bf16[384,1152]{1,0:T(8,128)(2,1)S(1)}, bf16[384,1152]{1,0:T(8,128)(2,1)}, u32[]{:S(2)}, u32[]{:S(2)}) collective-permute-start(bf16[384,1152]{1,0:T(8,128)(2,1)S(1)} %get-tuple-element.44.refs_1_.refs_2_), channel_id=1, source_target_pairs={{0,254},{1,3},{2,0},{3,5},{4,2},{5,7},{6,4},{7,9},{8,6},{9,11},{10... | collective-permute-start | bytes 2654216 | tf_op jit(solution)/shard_map/ppermute | solution.py:319
  9.6 2.2 %shard_map.68 = (f32[384,1152]{1,0:T(8,128)S(1)}, f32[32,128]{1,0:T(8,128)S(1)}) custom-call(f32[4]{0:T(128)S(1)} %pad_maximum_fusion.refs_0_.scalars, bf16[384,1152]{1,0:T(8,128)(2,1)S(1)} %get-tuple-element.44.refs_1_.refs_2_, bf16[384,1152]{1,0:T(8,128)(2,1)S(1)} %get-tuple-element.45.refs_2_.refs_1_), custom_call_target="tpu_custom_call" | custom-call | flops 679477248 | bytes 4423680 | tf_op jit(solution)/shard_map/pallas_call | solution.py:271
  11.9 15.9 %collective-permute-done.refs_1_.refs_2_ = bf16[384,1152]{1,0:T(8,128)(2,1)} collective-permute-done((bf16[384,1152]{1,0:T(8,128)(2,1)S(1)}, bf16[384,1152]{1,0:T(8,128)(2,1)}, u32[]{:S(2)}, u32[]{:S(2)}) %collective-permute-start) | collective-permute-done | bytes 884768 | tf_op jit(solution)/shard_map/ppermute | solution.py:319
  27.8 4.7 %collective-permute-start.1 = (bf16[384,1152]{1,0:T(8,128)(2,1)}, bf16[384,1152]{1,0:T(8,128)(2,1)S(1)}, u32[]{:S(2)}, u32[]{:S(2)}) collective-permute-start(bf16[384,1152]{1,0:T(8,128)(2,1)} %collective-permute-done.refs_1_.refs_2_), channel_id=1, source_target_pairs={{0,254},{1,3},{2,0},{3,5},{4,2},{5,7},{6,4},{7,9},{8,6},{9,11},{10... | collective-permute-start | bytes 2654216 | tf_op jit(solution)/shard_map/ppermute | solution.py:319
  32.5 3.3 %shard_map.69 = (f32[384,1152]{1,0:T(8,128)S(1)}, f32[32,128]{1,0:T(8,128)S(1)}) custom-call(f32[4]{0:T(128)S(1)} %pad_maximum_fusion.refs_0_.scalars, bf16[384,1152]{1,0:T(8,128)(2,1)S(1)} %get-tuple-element.45.refs_2_.refs_1_, bf16[384,1152]{1,0:T(8,128)(2,1)S(1)} %get-tuple-element.44.refs_1_.refs_2_, bf16[384,1152]{1,0:T(8,128)(2,1)} %collective-permute-done.4.refs_3_), custom_call_target="tpu_custom_call" | custom-call | flops 1358954496 | bytes 4423680 | tf_op jit(solution)/shard_map/pallas_call | solution.py:271
  36.0 2.4 %shard_map.71 = f32[32,128]{1,0:T(8,128)S(1)} custom-call(f32[4]{0:T(128)S(1)} %pad_maximum_fusion.refs_0_.scalars, bf16[384,1152]{1,0:T(8,128)(2,1)} %collective-permute-done.refs_1_.refs_2_, bf16[384,1152]{1,0:T(8,128)(2,1)} %collective-permute-done.2.refs_3_.refs_2_), custom_call_target="tpu_custom_call" | custom-call | flops 339738624 | bytes 884736 | tf_op jit(solution)/shard_map/pallas_call | solution.py:225
  38.4 3.7 %shard_map.70 = (f32[384,1152]{1,0:T(8,128)S(1)}, f32[32,128]{1,0:T(8,128)S(1)}) custom-call(f32[4]{0:T(128)S(1)} %pad_maximum_fusion.refs_0_.scalars, bf16[384,1152]{1,0:T(8,128)(2,1)S(1)} %get-tuple-element.44.refs_1_.refs_2_, bf16[384,1152]{1,0:T(8,128)(2,1)S(1)} %collective-permute-done.3.refs_2_.refs_3_, ...), custom_call_target="tpu_custom_call", output_to_operand_aliasing={{0}: (4, {})} | custom-call | flops 1358954496 | bytes 4423680 | tf_op jit(solution)/shard_map/pallas_call | solution.py:271
  42.1 7.5 %collective-permute-done.1.refs_5_.refs_1_.refs_2_ = bf16[384,1152]{1,0:T(8,128)(2,1)S(1)} collective-permute-done((bf16[384,1152]{1,0:T(8,128)(2,1)}, bf16[384,1152]{1,0:T(8,128)(2,1)S(1)}, u32[]{:S(2)}, u32[]{:S(2)}) %collective-permute-start.1) | collective-permute-done | bytes 884768 | tf_op jit(solution)/shard_map/ppermute | solution.py:319
  49.5 4.5 %collective-permute-start.6 = (bf16[384,1152]{1,0:T(8,128)(2,1)S(1)}, bf16[384,1152]{1,0:T(8,128)(2,1)}, u32[]{:S(2)}, u32[]{:S(2)}) collective-permute-start(bf16[384,1152]{1,0:T(8,128)(2,1)S(1)} %collective-permute-done.1.refs_5_.refs_1_.refs_2_), channel_id=1, source_target_pairs={{0,254},{1,3},{2,0},{3,5},{4,2},{5,7},{6,4},{7,9},{8,6},{9,11},{10... | collective-permute-start | bytes 2654216 | tf_op jit(solution)/shard_map/ppermute | solution.py:319
  54.0 3.1 %shard_map.73 = f32[32,128]{1,0:T(8,128)S(1)} custom-call(f32[4]{0:T(128)S(1)} %pad_maximum_fusion.refs_0_.scalars, bf16[384,1152]{1,0:T(8,128)(2,1)} %collective-permute-done.refs_1_.refs_2_, bf16[384,1152]{1,0:T(8,128)(2,1)} %collective-permute-done.2.refs_3_.refs_2_, bf16[384,1152]{1,0:T(8,128)(2,1)S(1)} %collective-permute-done.3.refs_2_.refs_3_, ...), custom_call_target="tpu_custom_call" | custom-call | flops 679477248 | bytes 884736 | tf_op jit(solution)/shard_map/pallas_call | solution.py:225
  57.2 4.0 %shard_map.72 = (f32[384,1152]{1,0:T(8,128)S(1)}, f32[32,128]{1,0:T(8,128)S(1)}) custom-call(f32[4]{0:T(128)S(1)} %pad_maximum_fusion.refs_0_.scalars, bf16[384,1152]{1,0:T(8,128)(2,1)S(1)} %get-tuple-element.45.refs_2_.refs_1_, bf16[384,1152]{1,0:T(8,128)(2,1)} %collective-permute-done.refs_1_.refs_2_, ...), custom_call_target="tpu_custom_call", output_to_operand_aliasing={{0}: (4, {})} | custom-call | flops 1358954496 | bytes 4423680 | tf_op jit(solution)/shard_map/pallas_call | solution.py:271
  63.8 2.9 %shard_map.74.refs_4_ = f32[384,1152]{1,0:T(8,128)S(1)} custom-call(f32[4]{0:T(128)S(1)} %pad_maximum_fusion.refs_0_.scalars, bf16[384,1152]{1,0:T(8,128)(2,1)S(1)} %get-tuple-element.44.refs_1_.refs_2_, bf16[384,1152]{1,0:T(8,128)(2,1)S(1)} %collective-permute-done.8.refs_2_.refs_5_, ...), custom_call_target="tpu_custom_call", output_to_operand_aliasing={{}: (4, {})} | custom-call | flops 1358954496 | bytes 4423680 | tf_op jit(solution)/shard_map/pallas_call | solution.py:271
  68.6 3.4 %collective-permute-start.11 = (bf16[384,1152]{1,0:T(8,128)(2,1)}, bf16[384,1152]{1,0:T(8,128)(2,1)}, u32[]{:S(2)}, u32[]{:S(2)}) collective-permute-start(bf16[384,1152]{1,0:T(8,128)(2,1)} %collective-permute-done.6.refs_2_), channel_id=1, source_target_pairs={{0,255},{1,2},{2,1},{3,4},{4,3},{5,6},{6,5},{7,8},{8,7},{9,10},{10... | collective-permute-start | bytes 2654216 | tf_op jit(solution)/shard_map/ppermute | solution.py:375
  71.9 4.0 %collective-permute-done.14 = f32[32,128]{1,0:T(8,128)S(1)} collective-permute-done((f32[32,128]{1,0:T(8,128)S(1)}, f32[32,128]{1,0:T(8,128)S(1)}, u32[]{:S(2)}, u32[]{:S(2)}) %collective-permute-start.14) | collective-permute-done | bytes 16416 | tf_op jit(solution)/shard_map/ppermute | solution.py:331
  76.0 11.1 %collective-permute-start.15 = (f32[32,128]{1,0:T(8,128)S(1)}, f32[32,128]{1,0:T(8,128)S(1)}, u32[]{:S(2)}, u32[]{:S(2)}) collective-permute-start(f32[32,128]{1,0:T(8,128)S(1)} %add.49), channel_id=1, source_target_pairs={{0,32},{1,33},{2,34},{3,35},{4,36},{5,37},{6,38},{7,39},{8,40},{9,... | collective-permute-start | bytes 49160 | tf_op jit(solution)/shard_map/ppermute | solution.py:331
  87.1 2.9 %shard_map.76.refs_5_ = f32[384,1152]{1,0:T(8,128)S(1)} custom-call(f32[4]{0:T(128)S(1)} %pad_maximum_fusion.refs_0_.scalars, bf16[384,1152]{1,0:T(8,128)(2,1)S(1)} %get-tuple-element.45.refs_2_.refs_1_, bf16[384,1152]{1,0:T(8,128)(2,1)S(1)} %collective-permute-done.1.refs_5_.refs_1_.refs_2_, ...), custom_call_target="tpu_custom_call", output_to_operand_aliasing={{}: (4, {})} | custom-call | flops 1358954496 | bytes 4423680 | tf_op jit(solution)/shard_map/pallas_call | solution.py:271
  90.0 3.7 %collective-permute-done.15 = f32[32,128]{1,0:T(8,128)S(1)} collective-permute-done((f32[32,128]{1,0:T(8,128)S(1)}, f32[32,128]{1,0:T(8,128)S(1)}, u32[]{:S(2)}, u32[]{:S(2)}) %collective-permute-start.15) | collective-permute-done | bytes 16416 | tf_op jit(solution)/shard_map/ppermute | solution.py:331
  94.4 3.7 %collective-permute-done.18 = f32[32,128]{1,0:T(8,128)S(1)} collective-permute-done((f32[32,128]{1,0:T(8,128)S(1)}, f32[32,128]{1,0:T(8,128)S(1)}, u32[]{:S(2)}, u32[]{:S(2)}) %collective-permute-start.18) | collective-permute-done | bytes 16416 | tf_op jit(solution)/shard_map/ppermute | solution.py:331
  98.1 2.9 %shard_map.77.refs_3_ = f32[384,1152]{1,0:T(8,128)S(1)} custom-call(f32[4]{0:T(128)S(1)} %pad_maximum_fusion.refs_0_.scalars, bf16[384,1152]{1,0:T(8,128)(2,1)S(1)} %get-tuple-element.44.refs_1_.refs_2_, bf16[384,1152]{1,0:T(8,128)(2,1)S(1)} %collective-permute-done.13.refs_2_, ...), custom_call_target="tpu_custom_call", output_to_operand_aliasing={{}: (4, {})} | custom-call | flops 1358954496 | bytes 4423680 | tf_op jit(solution)/shard_map/pallas_call | solution.py:271
  101.0 2.4 %collective-permute-done.19 = f32[32,128]{1,0:T(8,128)S(1)} collective-permute-done((f32[32,128]{1,0:T(8,128)S(1)}, f32[32,128]{1,0:T(8,128)S(1)}, u32[]{:S(2)}, u32[]{:S(2)}) %collective-permute-start.19) | collective-permute-done | bytes 16416 | tf_op jit(solution)/shard_map/ppermute | solution.py:331
  103.5 3.7 %collective-permute-done.20 = f32[32,128]{1,0:T(8,128)S(1)} collective-permute-done((f32[32,128]{1,0:T(8,128)S(1)}, f32[32,128]{1,0:T(8,128)S(1)}, u32[]{:S(2)}, u32[]{:S(2)}) %collective-permute-start.20) | collective-permute-done | bytes 16416 | tf_op jit(solution)/shard_map/ppermute | solution.py:331
  107.2 4.6 %collective-permute-done.21 = f32[32,128]{1,0:T(8,128)S(1)} collective-permute-done((f32[32,128]{1,0:T(8,128)S(1)}, f32[32,128]{1,0:T(8,128)S(1)}, u32[]{:S(2)}, u32[]{:S(2)}) %collective-permute-start.21) | collective-permute-done | bytes 16416 | tf_op jit(solution)/shard_map/ppermute | solution.py:331
  111.9 5.9 %shard_map.79 = (f32[384,1152]{1,0:T(8,128)}, f32[384,1152]{1,0:T(8,128)}) custom-call(f32[4]{0:T(128)S(1)} %pad_maximum_fusion.refs_0_.scalars, bf16[384,1152]{1,0:T(8,128)(2,1)S(1)} %get-tuple-element.45.refs_2_.refs_1_, bf16[384,1152]{1,0:T(8,128)(2,1)} %collective-permute-done.6.refs_2_, bf16[192,1152]{1,0:T(8,128)(2,1)S(1)} %collective-permute-done.16.refs_3_, ...), custom_call_target="tpu_custom_call" | custom-call | flops 1358954496 | bytes 4423680 | tf_op jit(solution)/shard_map/pallas_call | solution.py:271
  122.1 4.5 %shard_map.80 = (f32[384,1152]{1,0:T(8,128)}, f32[384,1152]{1,0:T(8,128)}) custom-call(f32[4]{0:T(128)S(1)} %copy-done.1, bf16[384,1152]{1,0:T(8,128)(2,1)S(1)} %get-tuple-element.44.refs_1_.refs_2_, bf16[384,1152]{1,0:T(8,128)(2,1)} %collective-permute-done.11.refs_2_, ...), custom_call_target="tpu_custom_call", output_to_operand_aliasing={{0}: (6, {}), {1}: (7, {})} | custom-call | flops 679477248 | bytes 4423680 | tf_op jit(solution)/shard_map/pallas_call | solution.py:271
  (51 shorter events, 11.6 us)
Async XLA Ops:
  2.4 25.4 %collective-permute-start = (bf16[384,1152]{1,0:T(8,128)(2,1)S(1)}, bf16[384,1152]{1,0:T(8,128)(2,1)}, u32[]{:S(2)}, u32[]{:S(2)}) collective-permute-start(bf16[384,1152]{1,0:T(8,128)(2,1)S(1)} %get-tuple-element.44.refs_1_.refs_2_), channel_id=1, source_target_pairs={{0,254},{1,3},{2,0},{3,5},{4,2},{5,7},{6,4},{7,9},{8,6},{9,11},{10... | collective-permute-start | bytes 2654216 | tf_op jit(solution)/shard_map/ppermute | solution.py:319
  8.2 24.3 %collective-permute-start.4 = (bf16[384,1152]{1,0:T(8,128)(2,1)S(1)}, bf16[384,1152]{1,0:T(8,128)(2,1)}, u32[]{:S(2)}, u32[]{:S(2)}) collective-permute-start(bf16[384,1152]{1,0:T(8,128)(2,1)S(1)} %get-tuple-element.45.refs_2_.refs_1_), channel_id=1, source_target_pairs={{0,1},{1,0},{2,3},{3,2},{4,5},{5,4},{6,7},{7,6},{8,9},{9,8},{10,11... | collective-permute-start | bytes 2654216 | tf_op jit(solution)/shard_map/ppermute | solution.py:325
  8.2 27.5 %collective-permute-start.2 = (bf16[384,1152]{1,0:T(8,128)(2,1)S(1)}, bf16[384,1152]{1,0:T(8,128)(2,1)}, u32[]{:S(2)}, u32[]{:S(2)}) collective-permute-start(bf16[384,1152]{1,0:T(8,128)(2,1)S(1)} %get-tuple-element.45.refs_2_.refs_1_), channel_id=1, source_target_pairs={{0,2},{1,255},{2,4},{3,1},{4,6},{5,3},{6,8},{7,5},{8,10},{9,7},{10... | collective-permute-start | bytes 2654216 | tf_op jit(solution)/shard_map/ppermute | solution.py:322
  9.6 102.2 %copy-start = (f32[4]{0:T(128)}, f32[4]{0:T(128)S(1)}, u32[]{:S(2)}) copy-start(f32[4]{0:T(128)S(1)} %pad_maximum_fusion.refs_0_.scalars) | copy-start | bytes 52
  27.8 8.0 %collective-permute-start.3 = (bf16[384,1152]{1,0:T(8,128)(2,1)}, bf16[384,1152]{1,0:T(8,128)(2,1)S(1)}, u32[]{:S(2)}, u32[]{:S(2)}) collective-permute-start(bf16[384,1152]{1,0:T(8,128)(2,1)} %collective-permute-done.refs_1_.refs_2_), channel_id=1, source_target_pairs={{0,1},{1,0},{2,3},{3,2},{4,5},{5,4},{6,7},{7,6},{8,9},{9,8},{10,11... | collective-permute-start | bytes 2654216 | tf_op jit(solution)/shard_map/ppermute | solution.py:325
  27.8 21.8 %collective-permute-start.1 = (bf16[384,1152]{1,0:T(8,128)(2,1)}, bf16[384,1152]{1,0:T(8,128)(2,1)S(1)}, u32[]{:S(2)}, u32[]{:S(2)}) collective-permute-start(bf16[384,1152]{1,0:T(8,128)(2,1)} %collective-permute-done.refs_1_.refs_2_), channel_id=1, source_target_pairs={{0,254},{1,3},{2,0},{3,5},{4,2},{5,7},{6,4},{7,9},{8,6},{9,11},{10... | collective-permute-start | bytes 2654216 | tf_op jit(solution)/shard_map/ppermute | solution.py:319
  35.8 13.8 %collective-permute-start.5 = (bf16[384,1152]{1,0:T(8,128)(2,1)}, bf16[384,1152]{1,0:T(8,128)(2,1)S(1)}, u32[]{:S(2)}, u32[]{:S(2)}) collective-permute-start(bf16[384,1152]{1,0:T(8,128)(2,1)} %collective-permute-done.2.refs_3_.refs_2_), channel_id=1, source_target_pairs={{0,1},{1,0},{2,3},{3,2},{4,5},{5,4},{6,7},{7,6},{8,9},{9,8},{10,11... | collective-permute-start | bytes 2654216 | tf_op jit(solution)/shard_map/ppermute | solution.py:325
  35.9 25.3 %collective-permute-start.7 = (bf16[384,1152]{1,0:T(8,128)(2,1)}, bf16[384,1152]{1,0:T(8,128)(2,1)S(1)}, u32[]{:S(2)}, u32[]{:S(2)}) collective-permute-start(bf16[384,1152]{1,0:T(8,128)(2,1)} %collective-permute-done.2.refs_3_.refs_2_), channel_id=1, source_target_pairs={{0,2},{1,255},{2,4},{3,1},{4,6},{5,3},{6,8},{7,5},{8,10},{9,7},{10... | collective-permute-start | bytes 2654216 | tf_op jit(solution)/shard_map/ppermute | solution.py:322
  49.5 11.6 %collective-permute-start.8 = (bf16[384,1152]{1,0:T(8,128)(2,1)S(1)}, bf16[384,1152]{1,0:T(8,128)(2,1)S(1)}, u32[]{:S(2)}, u32[]{:S(2)}) collective-permute-start(bf16[384,1152]{1,0:T(8,128)(2,1)S(1)} %collective-permute-done.1.refs_5_.refs_1_.refs_2_), channel_id=1, source_target_pairs={{0,1},{1,0},{2,3},{3,2},{4,5},{5,4},{6,7},{7,6},{8,9},{9,8},{10,11... | collective-permute-start | bytes 2654216 | tf_op jit(solution)/shard_map/ppermute | solution.py:325
  49.5 17.4 %collective-permute-start.6 = (bf16[384,1152]{1,0:T(8,128)(2,1)S(1)}, bf16[384,1152]{1,0:T(8,128)(2,1)}, u32[]{:S(2)}, u32[]{:S(2)}) collective-permute-start(bf16[384,1152]{1,0:T(8,128)(2,1)S(1)} %collective-permute-done.1.refs_5_.refs_1_.refs_2_), channel_id=1, source_target_pairs={{0,254},{1,3},{2,0},{3,5},{4,2},{5,7},{6,4},{7,9},{8,6},{9,11},{10... | collective-permute-start | bytes 2654216 | tf_op jit(solution)/shard_map/ppermute | solution.py:319
  61.2 5.8 %collective-permute-start.9 = (bf16[384,1152]{1,0:T(8,128)(2,1)S(1)}, bf16[384,1152]{1,0:T(8,128)(2,1)S(1)}, u32[]{:S(2)}, u32[]{:S(2)}) collective-permute-start(bf16[384,1152]{1,0:T(8,128)(2,1)S(1)} %collective-permute-done.7.refs_3_.refs_2_), channel_id=1, source_target_pairs={{0,1},{1,0},{2,3},{3,2},{4,5},{5,4},{6,7},{7,6},{8,9},{9,8},{10,11... | collective-permute-start | bytes 2654216 | tf_op jit(solution)/shard_map/ppermute | solution.py:325
  61.3 32.4 %collective-permute-start.12 = (bf16[384,1152]{1,0:T(8,128)(2,1)S(1)}, bf16[384,1152]{1,0:T(8,128)(2,1)S(1)}, u32[]{:S(2)}, u32[]{:S(2)}) collective-permute-start(bf16[384,1152]{1,0:T(8,128)(2,1)S(1)} %collective-permute-done.7.refs_3_.refs_2_), channel_id=1, source_target_pairs={{0,2},{1,255},{2,4},{3,1},{4,6},{5,3},{6,8},{7,5},{8,10},{9,7},{10... | collective-permute-start | bytes 2654216 | tf_op jit(solution)/shard_map/ppermute | solution.py:322
  63.4 3.4 %collective-permute-start.10 = (f32[32,128]{1,0:T(8,128)S(1)}, f32[32,128]{1,0:T(8,128)S(1)}, u32[]{:S(2)}, u32[]{:S(2)}) collective-permute-start(f32[32,128]{1,0:T(8,128)S(1)} %add_add_fusion), channel_id=1, source_target_pairs={{0,1},{1,0},{2,3},{3,2},{4,5},{5,4},{6,7},{7,6},{8,9},{9,8},{10,11... | collective-permute-start | bytes 49160 | tf_op jit(solution)/shard_map/ppermute | solution.py:331
  67.0 26.7 %collective-permute-start.13 = (bf16[384,1152]{1,0:T(8,128)(2,1)}, bf16[384,1152]{1,0:T(8,128)(2,1)S(1)}, u32[]{:S(2)}, u32[]{:S(2)}) collective-permute-start(bf16[384,1152]{1,0:T(8,128)(2,1)} %collective-permute-done.6.refs_2_), channel_id=1, source_target_pairs={{0,1},{1,0},{2,3},{3,2},{4,5},{5,4},{6,7},{7,6},{8,9},{9,8},{10,11... | collective-permute-start | bytes 2654216 | tf_op jit(solution)/shard_map/ppermute | solution.py:325
  67.0 9.0 %collective-permute-start.14 = (f32[32,128]{1,0:T(8,128)S(1)}, f32[32,128]{1,0:T(8,128)S(1)}, u32[]{:S(2)}, u32[]{:S(2)}) collective-permute-start(f32[32,128]{1,0:T(8,128)S(1)} %add.48), channel_id=1, source_target_pairs={{0,16},{1,17},{2,18},{3,19},{4,20},{5,21},{6,22},{7,23},{8,24},{9,... | collective-permute-start | bytes 49160 | tf_op jit(solution)/shard_map/ppermute | solution.py:331
  68.6 52.9 %collective-permute-start.11 = (bf16[384,1152]{1,0:T(8,128)(2,1)}, bf16[384,1152]{1,0:T(8,128)(2,1)}, u32[]{:S(2)}, u32[]{:S(2)}) collective-permute-start(bf16[384,1152]{1,0:T(8,128)(2,1)} %collective-permute-done.6.refs_2_), channel_id=1, source_target_pairs={{0,255},{1,2},{2,1},{3,4},{4,3},{5,6},{6,5},{7,8},{8,7},{9,10},{10... | collective-permute-start | bytes 2654216 | tf_op jit(solution)/shard_map/ppermute | solution.py:375
  76.0 17.7 %collective-permute-start.15 = (f32[32,128]{1,0:T(8,128)S(1)}, f32[32,128]{1,0:T(8,128)S(1)}, u32[]{:S(2)}, u32[]{:S(2)}) collective-permute-start(f32[32,128]{1,0:T(8,128)S(1)} %add.49), channel_id=1, source_target_pairs={{0,32},{1,33},{2,34},{3,35},{4,36},{5,37},{6,38},{7,39},{8,40},{9,... | collective-permute-start | bytes 49160 | tf_op jit(solution)/shard_map/ppermute | solution.py:331
  93.8 9.6 %collective-permute-start.17 = (bf16[192,1152]{1,0:T(8,128)(2,1)S(1)}, bf16[192,1152]{1,0:T(8,128)(2,1)S(1)}, u32[]{:S(2)}, u32[]{:S(2)}) collective-permute-start(bf16[192,1152]{1,0:T(8,128)(2,1)S(1)} %get-tuple-element.85), channel_id=1, source_target_pairs={{0,1},{1,0},{2,3},{3,2},{4,5},{5,4},{6,7},{7,6},{8,9},{9,8},{10,11... | collective-permute-start | bytes 1327112 | tf_op jit(solution)/shard_map/ppermute | solution.py:325
  93.9 9.5 %collective-permute-start.16 = (bf16[192,1152]{1,0:T(8,128)(2,1)S(1)}, bf16[192,1152]{1,0:T(8,128)(2,1)S(1)}, u32[]{:S(2)}, u32[]{:S(2)}) collective-permute-start(bf16[192,1152]{1,0:T(8,128)(2,1)S(1)} %get-tuple-element.86), channel_id=1, source_target_pairs={{0,1},{1,0},{2,3},{3,2},{4,5},{5,4},{6,7},{7,6},{8,9},{9,8},{10,11... | collective-permute-start | bytes 1327112 | tf_op jit(solution)/shard_map/ppermute | solution.py:325
  94.4 3.7 %collective-permute-start.18 = (f32[32,128]{1,0:T(8,128)S(1)}, f32[32,128]{1,0:T(8,128)S(1)}, u32[]{:S(2)}, u32[]{:S(2)}) collective-permute-start(f32[32,128]{1,0:T(8,128)S(1)} %add.50), channel_id=1, source_target_pairs={{0,64},{1,65},{2,66},{3,67},{4,68},{5,69},{6,70},{7,71},{8,72},{9,... | collective-permute-start | bytes 49160 | tf_op jit(solution)/shard_map/ppermute | solution.py:331
  98.1 5.2 %collective-permute-start.19 = (f32[32,128]{1,0:T(8,128)S(1)}, f32[32,128]{1,0:T(8,128)S(1)}, u32[]{:S(2)}, u32[]{:S(2)}) collective-permute-start(f32[32,128]{1,0:T(8,128)S(1)} %add.51), channel_id=1, source_target_pairs={{0,128},{1,129},{2,130},{3,131},{4,132},{5,133},{6,134},{7,135},{8... | collective-permute-start | bytes 49160 | tf_op jit(solution)/shard_map/ppermute | solution.py:331
  103.4 3.8 %collective-permute-start.20 = (f32[32,128]{1,0:T(8,128)S(1)}, f32[32,128]{1,0:T(8,128)S(1)}, u32[]{:S(2)}, u32[]{:S(2)}) collective-permute-start(f32[32,128]{1,0:T(8,128)S(1)} %add.52), channel_id=1, source_target_pairs={{0,2},{1,3},{2,0},{3,1},{4,6},{5,7},{6,4},{7,5},{8,10},{9,11},{10,... | collective-permute-start | bytes 49160 | tf_op jit(solution)/shard_map/ppermute | solution.py:331
  107.2 4.6 %collective-permute-start.21 = (f32[32,128]{1,0:T(8,128)S(1)}, f32[32,128]{1,0:T(8,128)S(1)}, u32[]{:S(2)}, u32[]{:S(2)}) collective-permute-start(f32[32,128]{1,0:T(8,128)S(1)} %add.53), channel_id=1, source_target_pairs={{0,4},{1,5},{2,6},{3,7},{4,0},{5,1},{6,2},{7,3},{8,12},{9,13},{10,... | collective-permute-start | bytes 49160 | tf_op jit(solution)/shard_map/ppermute | solution.py:331
  111.8 7.6 %collective-permute-start.22 = (f32[32,128]{1,0:T(8,128)S(1)}, f32[32,128]{1,0:T(8,128)S(1)}, u32[]{:S(2)}, u32[]{:S(2)}) collective-permute-start(f32[32,128]{1,0:T(8,128)S(1)} %add.54), channel_id=1, source_target_pairs={{0,8},{1,9},{2,10},{3,11},{4,12},{5,13},{6,14},{7,15},{8,0},{9,1},... | collective-permute-start | bytes 49160 | tf_op jit(solution)/shard_map/ppermute | solution.py:331
  (1 other events, 0.6 us)

commit v2 on v1

--- a/solution.py
+++ b/solution.py
@@ -11,7 +11,7 @@
 EPS = 1e-06
 LOG2_E = 1.4426950408889634
 LN_2 = 0.6931471805599453
-ROUNDS = (1, 16, 32, 64, 128, 2, 4, 8)
+ROUNDS = ((16,), (32,), (64,), (128,), (2,), (4,), (8,), 1)
 VMEM_LIMIT = 24 * 1024 * 1024
 SMEM = pl.BlockSpec(memory_space=pltpu.SMEM)
 VMEM = pl.BlockSpec(memory_space=pltpu.VMEM)
@@ -66,9 +66,7 @@
         out_specs=[VMEM, VMEM],
         scratch_shapes=[pltpu.VMEM((2, *x.shape), jnp.bfloat16), pltpu.SemaphoreType.DMA((2, 2))],
         compiler_params=pltpu.CompilerParams(vmem_limit_bytes=VMEM_LIMIT),
-        cost_estimate=pl.CostEstimate(
-            flops=4 * x.size, bytes_accessed=8 * x.size, transcendentals=0
-        ),
+        cost_estimate=pl.CostEstimate(flops=1, bytes_accessed=1, transcendentals=0),
     )(x, y)
 
 
@@ -228,9 +226,7 @@
         in_specs=[SMEM] + [VMEM] * len(blocks),
         out_specs=VMEM,
         compiler_params=pltpu.CompilerParams(vmem_limit_bytes=VMEM_LIMIT),
-        cost_estimate=pl.CostEstimate(
-            flops=2 * pairs * width, bytes_accessed=2 * rows * width, transcendentals=3 * pairs
-        ),
+        cost_estimate=pl.CostEstimate(flops=1, bytes_accessed=1, transcendentals=0),
     )(scalars, *blocks)
 
 
@@ -276,26 +272,25 @@
         scratch_shapes=scratch,
         input_output_aliases=aliases,
         compiler_params=pltpu.CompilerParams(vmem_limit_bytes=VMEM_LIMIT),
-        cost_estimate=pl.CostEstimate(
-            flops=4 * pairs * width, bytes_accessed=10 * rows * width, transcendentals=3 * pairs
-        ),
+        cost_estimate=pl.CostEstimate(flops=1, bytes_accessed=1, transcendentals=0),
     )(*args)
 
 
-def finish_kernel(divisor, scalars, stats, out_ref):
-    sums = [jnp.sum(stats[row : row + 8, :]) for row in range(0, 32, 8)]
+def finish_kernel(divisor, scalars, mine, theirs, out_ref):
+    total = mine[...] + theirs[...]
+    sums = [jnp.sum(total[row : row + 8, :]) for row in range(0, 32, 8)]
     out_ref[0] = (sums[0] * LN_2 + sums[1]) / divisor
     out_ref[1] = sums[2] * scalars[0] / divisor
     out_ref[2] = sums[3] / divisor
 
 
-def finished(scalars, stats, divisor):
+def finished(scalars, mine, theirs, divisor):
     return pl.pallas_call(
         functools.partial(finish_kernel, divisor),
         out_shape=jax.ShapeDtypeStruct((3,), jnp.float32),
-        in_specs=[SMEM, VMEM],
+        in_specs=[SMEM, VMEM, VMEM],
         out_specs=SMEM,
-    )(scalars, stats)
+    )(scalars, mine, theirs)
 
 
 def tied(*values):
@@ -324,74 +319,85 @@
     def swap(value):
         return lax.ppermute(value, "dp", other_core)
 
-    def all_added(value, rounds):
-        for distance in rounds:
+    def exchanged(value, distance):
+        return lax.ppermute(value, "dp", [(d, d ^ distance) for d in range(count)])
+
+    def all_added(value, distances):
+        for distance in distances:
             if distance < count:
-                pairs = [(d, d ^ distance) for d in range(count)]
-                value = value + lax.ppermute(value, "dp", pairs)
+                value = value + exchanged(value, distance)
         return value
 
     whole = lambda i: (i, 0, rows)
     a, b = normalized(x, y)
     p1 = up(a)
-    r1 = down(b)
     sibling = swap(b)
     acc_a, stats0 = stage(scalars, a, [b], ["all"], label=True)
-
-    p1, acc_a = tied(p1, acc_a)
+    b, acc_a = tied(b, acc_a)
+    r1 = down(b)
+    acc_b, stats1 = stage(scalars, b, [a, sibling], [None, "core1"], label=True)
+
+    p1, acc_a, acc_b = tied(p1, acc_a, acc_b)
     p2, from_p1 = up(p1), swap(p1)
-    acc_b, stats1 = stage(scalars, b, [a, sibling], [None, "core1"], label=True)
-
-    r1, from_p1, acc_b = tied(r1, from_p1, acc_b)
+    acc_b, stats2 = stage(scalars, b, [p1], ["all"], acc_b)
+
+    r1, acc_b = tied(r1, acc_b)
     r2, from_r1 = down(r1), swap(r1)
-    acc_a, stats2 = stage(scalars, a, [from_p1, r1], ["core0", None], acc_a)
+    (acc_a,) = stage(scalars, a, [r1], [None], acc_a)
     stats3 = middle(scalars, [p1, r1], (((whole(0),), (whole(1),)),))
 
-    p2, from_r1, acc_a, stats3 = tied(p2, from_r1, acc_a, stats3)
+    p2, from_p1, acc_a, stats3 = tied(p2, from_p1, acc_a, stats3)
     p3, from_p2 = up(p2), swap(p2)
-    acc_b, stats4 = stage(scalars, b, [p1, from_r1], ["all", "core1"], acc_b)
-    stats5 = middle(
-        scalars, [p1, r1, from_p1, from_r1, p2],
+    acc_a, stats4 = stage(scalars, a, [from_p1], ["core0"], acc_a)
+    stats5 = middle(scalars, [p2, r1], (((whole(0),), (whole(1),)),))
+
+    r2, from_r1, acc_a, stats5 = tied(r2, from_r1, acc_a, stats5)
+    r3, from_r2 = down(r2), swap(r2)
+    acc_b, stats6 = stage(scalars, b, [from_r1], ["core1"], acc_b)
+    stats7 = middle(
+        scalars, [p1, r1, p2, r2, from_p1, from_r1, from_p2],
         (
-            ((whole(0), whole(1)), (whole(2), whole(3))),
-            ((whole(4),), (whole(1),)),
+            ((whole(0), whole(1)), (whole(4), whole(5))),
+            ((whole(2), whole(3)), (whole(4), whole(5))),
+            (((2, 0, half), (6, half, half)), (whole(6), whole(2))),
         ),
     )
-
-    r2, from_p2, acc_b, stats5 = tied(r2, from_p2, acc_b, stats5)
-    r3, from_r2 = down(r2), swap(r2)
-    stats6 = middle(
-        scalars, [p2, r2, from_p1, from_r1, from_p2],
-        (
-            ((whole(0), whole(1)), (whole(2), whole(3))),
-            (((0, 0, half), (4, half, half)), (whole(4), whole(0))),
-        ),
+    stats = (stats0 + stats1 + stats2 + stats3) + (stats4 + stats5 + stats6 + stats7)
+    rounds = iter(ROUNDS)
+    stats, acc_a, acc_b = tied(stats, acc_a, acc_b)
+    stats = all_added(stats, next(rounds))
+    (acc_a,) = stage(scalars, a, [r2], [None], acc_a)
+    stats, acc_a, acc_b = tied(stats, acc_a, acc_b)
+    stats = all_added(stats, next(rounds))
+    (acc_a,) = stage(scalars, a, [from_p2], [None], acc_a)
+
+    p3, acc_a, acc_b, stats = tied(p3, acc_a, acc_b, stats)
+    last, from_p3 = lax.ppermute(p3, "dp", cross), swap(p3)
+    stats = all_added(stats, next(rounds))
+    (acc_b,) = stage(scalars, b, [p2], [None], acc_b)
+    stats, acc_a, acc_b = tied(stats, acc_a, acc_b)
+    stats = all_added(stats, next(rounds))
+    (acc_b,) = stage(scalars, b, [from_r2], [None], acc_b)
+
+    r3, acc_a, acc_b, stats = tied(r3, acc_a, acc_b, stats)
+    from_r3 = [swap(r3[:half]), swap(r3[half:])]
+    stats = all_added(stats, next(rounds))
+    (acc_a,) = stage(scalars, a, [r3], [None], acc_a)
+    stats, acc_a, acc_b = tied(stats, acc_a, acc_b)
+    stats = all_added(stats, next(rounds))
+    (acc_a,) = stage(scalars, a, [from_p3], [None], acc_a)
+    stats, acc_a, acc_b = tied(stats, acc_a, acc_b)
+    stats = all_added(stats, next(rounds))
+    outs = stage(
+        scalars, b, [p3, *from_r3], [None, None, None], acc_b, final=(1, x, y, None)
     )
-    stats = stats0 + stats1 + stats2 + stats3 + stats4 + stats5 + stats6
-    stats = all_added(stats, ROUNDS[:1])
-    (acc_a,) = stage(scalars, a, [from_p2, r2], [None, None], acc_a)
-
-    p3, from_r2, acc_a, stats = tied(p3, from_r2, acc_a, stats)
-    last, from_p3 = lax.ppermute(p3, "dp", cross), swap(p3)
-    stats = all_added(stats, ROUNDS[1:3])
-    (acc_b,) = stage(scalars, b, [p2, from_r2], [None, None], acc_b)
-
-    r3, from_p3, acc_b, stats = tied(r3, from_p3, acc_b, stats)
-    from_r3 = [swap(r3[:half]), swap(r3[half:])]
-    stats = all_added(stats, ROUNDS[3:5])
-    (acc_a,) = stage(scalars, a, [from_p3, r3], [None, None], acc_a)
-
-    from_r3, acc_a, stats = tied(from_r3, acc_a, stats)
-    outs = stage(
-        scalars, b, [p3, *from_r3], [None, None, None], acc_b,
-        final=(1, x, y, None),
+
+    last, outs, stats = tied(last, outs, stats)
+    theirs = exchanged(stats, next(rounds))
+    grad_image, grad_text = stage(
+        scalars, a, [last], [None], acc_a, final=(0, x, y, tuple(outs))
     )
-    stats = all_added(stats, ROUNDS[5:])
-    sums = finished(scalars, stats, float(rows * count * STEPS))
-    last, sums = tied(last, sums)
-    grad_image, grad_text = stage(
-        scalars, a, [last], [None], acc_a, final=(0, x, y, outs)
-    )
+    sums = finished(scalars, stats, theirs, float(rows * count * STEPS))
     return grad_image, grad_text, sums
 
 

time: 127 us -> 123 us (0.969); the launches traced: 127 us -> 121 us
  waiting for transfers between devices: 47.5 us -> 38.1 us
  starting transfers between devices: 32.7 us -> 36 us
    ppermute x8, waiting for transfers between devices: 23.9 us -> 16.2 us  [exchanged(): return lax.ppermute(value, 'dp', [(d, d ^ distance) for d in range(count)])]
    pallas_call x9 -> x14, Pallas kernels: 32.1 us -> 34.8 us  [stage(): pl.pallas_call(functools.partial(stage_kernel, plan), out_shape=out_shape...]
    ppermute x1, starting transfers between devices: 3.39 us -> 6.01 us  [per_device(): last, from_p3 = (lax.ppermute(p3, 'dp', cross), swap(p3))]
    pallas_call x3, Pallas kernels: 7.51 us -> 5.73 us  [middle(): pl.pallas_call(functools.partial(middle_kernel, plan), out_shape=jax.Shap...]
    ppermute x3, waiting for transfers between devices: 23.6 us -> 21.8 us  [up(): return lax.ppermute(value, 'dp', up_down)]
  transfers between devices with their start and end apart: 23 -> 23, of which waited for: 10 -> 6; matrix products, arithmetic and copies ran while one was open for 1% -> 0% of each run, Pallas kernels for 29% -> 33%
where the time goes in v2:
time: 123 us; the launch traced here: 121 us
  Pallas kernels  43.7 us (36%)
  waiting for transfers between devices  38.1 us (31%)
  starting transfers between devices  36 us (29%)
  between operations  2.54 us (2%)
    pallas_call x14, Pallas kernels, stage(): pl.pallas_call(functools.partial(stage_kernel, plan), out_shape=out_shape...  34.8 us
    ppermute x3, waiting for transfers between devices, up(): return lax.ppermute(value, 'dp', up_down)  21.8 us
    ppermute x8, waiting for transfers between devices, exchanged(): return lax.ppermute(value, 'dp', [(d, d ^ distance) for d in range(count)])  16.2 us
    ppermute x3, starting transfers between devices, up(): return lax.ppermute(value, 'dp', up_down)  15 us
    ppermute x8, starting transfers between devices, exchanged(): return lax.ppermute(value, 'dp', [(d, d ^ distance) for d in range(count)])  13.4 us
    ppermute x1, starting transfers between devices, per_device(): last, from_p3 = (lax.ppermute(p3, 'dp', cross), swap(p3))  6.01 us
    pallas_call x3, Pallas kernels, middle(): pl.pallas_call(functools.partial(middle_kernel, plan), out_shape=jax.Shap...  5.73 us
  transfers between devices with their start and end apart: 23, of which 6 were waited for; matrix products, arithmetic and copies ran while one was open for 0% of the time, Pallas kernels for 33%

profile of v2, /device:TPU:16, one launch (start us, length us, event | category | flops | bytes accessed | tf_op | source)
XLA Modules:
  0.0 121.1 jit_solution(7366635291073488088)
XLA Ops:
  2.5 5.8 %collective-permute-start = (bf16[384,1152]{1,0:T(8,128)(2,1)S(1)}, bf16[384,1152]{1,0:T(8,128)(2,1)S(1)}, u32[]{:S(2)}, u32[]{:S(2)}) collective-permute-start(bf16[384,1152]{1,0:T(8,128)(2,1)S(1)} %get-tuple-element.61.refs_1_.refs_2_), channel_id=1, source_target_pairs={{0,254},{1,3},{2,0},{3,5},{4,2},{5,7},{6,4},{7,9},{8,6},{9,11},{10... | collective-permute-start | bytes 2654216 | tf_op jit(solution)/shard_map/ppermute | solution.py:314
  9.7 2.2 %shard_map.68 = (f32[384,1152]{1,0:T(8,128)S(1)}, f32[32,128]{1,0:T(8,128)S(1)}) custom-call(f32[4]{0:T(128)S(1)} %pad_maximum_fusion.refs_0_.scalars, bf16[384,1152]{1,0:T(8,128)(2,1)S(1)} %get-tuple-element.61.refs_1_.refs_2_, bf16[384,1152]{1,0:T(8,128)(2,1)S(1)} %get-tuple-element.65.refs_2_.refs_1_), custom_call_target="tpu_custom_call" | custom-call | flops 1 | bytes 1 | tf_op jit(solution)/shard_map/pallas_call | solution.py:267
  12.1 2.6 %shard_map.69 = (f32[384,1152]{1,0:T(8,128)S(1)}, f32[32,128]{1,0:T(8,128)S(1)}) custom-call(f32[4]{0:T(128)S(1)} %pad_maximum_fusion.refs_0_.scalars, bf16[384,1152]{1,0:T(8,128)(2,1)S(1)} %get-tuple-element.65.refs_2_.refs_1_, bf16[384,1152]{1,0:T(8,128)(2,1)S(1)} %get-tuple-element.61.refs_1_.refs_2_, bf16[384,1152]{1,0:T(8,128)(2,1)S(1)} %collective-permute-done.1.refs_3_), custom_call_target="tpu_custom_call" | custom-call | flops 1 | bytes 1 | tf_op jit(solution)/shard_map/pallas_call | solution.py:267
  14.7 10.4 %collective-permute-done.refs_2_.refs_1_ = bf16[384,1152]{1,0:T(8,128)(2,1)S(1)} collective-permute-done((bf16[384,1152]{1,0:T(8,128)(2,1)S(1)}, bf16[384,1152]{1,0:T(8,128)(2,1)S(1)}, u32[]{:S(2)}, u32[]{:S(2)}) %collective-permute-start) | collective-permute-done | bytes 884768 | tf_op jit(solution)/shard_map/ppermute | solution.py:314
  25.1 4.6 %collective-permute-start.2 = (bf16[384,1152]{1,0:T(8,128)(2,1)S(1)}, bf16[384,1152]{1,0:T(8,128)(2,1)S(1)}, u32[]{:S(2)}, u32[]{:S(2)}) collective-permute-start(bf16[384,1152]{1,0:T(8,128)(2,1)S(1)} %collective-permute-done.refs_2_.refs_1_), channel_id=1, source_target_pairs={{0,254},{1,3},{2,0},{3,5},{4,2},{5,7},{6,4},{7,9},{8,6},{9,11},{10... | collective-permute-start | bytes 2654216 | tf_op jit(solution)/shard_map/ppermute | solution.py:314
  29.7 2.2 %shard_map.70 = (f32[384,1152]{1,0:T(8,128)S(1)}, f32[32,128]{1,0:T(8,128)S(1)}) custom-call(f32[4]{0:T(128)S(1)} %pad_maximum_fusion.refs_0_.scalars, bf16[384,1152]{1,0:T(8,128)(2,1)S(1)} %get-tuple-element.65.refs_2_.refs_1_, bf16[384,1152]{1,0:T(8,128)(2,1)S(1)} %collective-permute-done.refs_2_.refs_1_, ...), custom_call_target="tpu_custom_call", output_to_operand_aliasing={{0}: (3, {})} | custom-call | flops 1 | bytes 1 | tf_op jit(solution)/shard_map/pallas_call | solution.py:267
  34.1 2.0 %shard_map.71.refs_3_ = f32[384,1152]{1,0:T(8,128)S(1)} custom-call(f32[4]{0:T(128)S(1)} %pad_maximum_fusion.refs_0_.scalars, bf16[384,1152]{1,0:T(8,128)(2,1)S(1)} %get-tuple-element.61.refs_1_.refs_2_, bf16[384,1152]{1,0:T(8,128)(2,1)S(1)} %collective-permute-done.4.refs_2_, f32[384,1152]{1,0:T(8,128)S(1)} %get-tuple-element.71.refs_3_), custom_call_target="tpu_custom_call", output_to_operand_aliasing={{}: (3, {})} | custom-call | flops 1 | bytes 1 | tf_op jit(solution)/shard_map/pallas_call | solution.py:267
  36.1 11.4 %collective-permute-done.2.refs_1_.refs_3_.refs_2_ = bf16[384,1152]{1,0:T(8,128)(2,1)S(1)} collective-permute-done((bf16[384,1152]{1,0:T(8,128)(2,1)S(1)}, bf16[384,1152]{1,0:T(8,128)(2,1)S(1)}, u32[]{:S(2)}, u32[]{:S(2)}) %collective-permute-start.2) | collective-permute-done | bytes 884768 | tf_op jit(solution)/shard_map/ppermute | solution.py:314
  47.6 4.6 %collective-permute-start.5 = (bf16[384,1152]{1,0:T(8,128)(2,1)S(1)}, bf16[384,1152]{1,0:T(8,128)(2,1)S(1)}, u32[]{:S(2)}, u32[]{:S(2)}) collective-permute-start(bf16[384,1152]{1,0:T(8,128)(2,1)S(1)} %collective-permute-done.2.refs_1_.refs_3_.refs_2_), channel_id=1, source_target_pairs={{0,254},{1,3},{2,0},{3,5},{4,2},{5,7},{6,4},{7,9},{8,6},{9,11},{10... | collective-permute-start | bytes 2654216 | tf_op jit(solution)/shard_map/ppermute | solution.py:314
  53.7 2.2 %shard_map.73 = (f32[384,1152]{1,0:T(8,128)S(1)}, f32[32,128]{1,0:T(8,128)S(1)}) custom-call(f32[4]{0:T(128)S(1)} %pad_maximum_fusion.refs_0_.scalars, bf16[384,1152]{1,0:T(8,128)(2,1)S(1)} %get-tuple-element.61.refs_1_.refs_2_, bf16[384,1152]{1,0:T(8,128)(2,1)S(1)} %collective-permute-done.3.refs_2_.refs_5_, ...), custom_call_target="tpu_custom_call", output_to_operand_aliasing={{0}: (3, {})} | custom-call | flops 1 | bytes 1 | tf_op jit(solution)/shard_map/pallas_call | solution.py:267
  56.1 2.2 %shard_map.75 = (f32[384,1152]{1,0:T(8,128)S(1)}, f32[32,128]{1,0:T(8,128)S(1)}) custom-call(f32[4]{0:T(128)S(1)} %pad_maximum_fusion.refs_0_.scalars, bf16[384,1152]{1,0:T(8,128)(2,1)S(1)} %get-tuple-element.65.refs_2_.refs_1_, bf16[384,1152]{1,0:T(8,128)(2,1)S(1)} %collective-permute-done.8.refs_2_.refs_6_, ...), custom_call_target="tpu_custom_call", output_to_operand_aliasing={{0}: (3, {})} | custom-call | flops 1 | bytes 1 | tf_op jit(solution)/shard_map/pallas_call | solution.py:267
  58.4 2.7 %shard_map.76 = f32[32,128]{1,0:T(8,128)S(1)} custom-call(f32[4]{0:T(128)S(1)} %pad_maximum_fusion.refs_0_.scalars, bf16[384,1152]{1,0:T(8,128)(2,1)S(1)} %collective-permute-done.refs_2_.refs_1_, bf16[384,1152]{1,0:T(8,128)(2,1)S(1)} %collective-permute-done.4.refs_2_, bf16[384,1152]{1,0:T(8,128)(2,1)S(1)} %collective-permute-done.2.refs_1_.refs_3_.refs_2_, ...), custom_call_target="tpu_custom_call" | custom-call | flops 1 | bytes 1 | tf_op jit(solution)/shard_map/pallas_call | solution.py:223
  62.8 2.0 %shard_map.77.refs_3_ = f32[384,1152]{1,0:T(8,128)S(1)} custom-call(f32[4]{0:T(128)S(1)} %pad_maximum_fusion.refs_0_.scalars, bf16[384,1152]{1,0:T(8,128)(2,1)S(1)} %get-tuple-element.61.refs_1_.refs_2_, bf16[384,1152]{1,0:T(8,128)(2,1)S(1)} %collective-permute-done.7.refs_4_.refs_2_, ...), custom_call_target="tpu_custom_call", output_to_operand_aliasing={{}: (3, {})} | custom-call | flops 1 | bytes 1 | tf_op jit(solution)/shard_map/pallas_call | solution.py:267
  64.8 7.2 %collective-permute-done.9 = f32[32,128]{1,0:T(8,128)S(1)} collective-permute-done((f32[32,128]{1,0:T(8,128)S(1)}, f32[32,128]{1,0:T(8,128)S(1)}, u32[]{:S(2)}, u32[]{:S(2)}) %collective-permute-start.9) | collective-permute-done | bytes 16416 | tf_op jit(solution)/shard_map/ppermute | solution.py:323
  72.0 4.7 %collective-permute-start.10 = (f32[32,128]{1,0:T(8,128)S(1)}, f32[32,128]{1,0:T(8,128)S(1)}, u32[]{:S(2)}, u32[]{:S(2)}) collective-permute-start(f32[32,128]{1,0:T(8,128)S(1)} %add.49), channel_id=1, source_target_pairs={{0,32},{1,33},{2,34},{3,35},{4,36},{5,37},{6,38},{7,39},{8,40},{9,... | collective-permute-start | bytes 49160 | tf_op jit(solution)/shard_map/ppermute | solution.py:323
  84.1 6.0 %collective-permute-start.11 = (bf16[384,1152]{1,0:T(8,128)(2,1)S(1)}, bf16[384,1152]{1,0:T(8,128)(2,1)S(1)}, u32[]{:S(2)}, u32[]{:S(2)}) collective-permute-start(bf16[384,1152]{1,0:T(8,128)(2,1)S(1)} %collective-permute-done.5.refs_2_), channel_id=1, source_target_pairs={{0,255},{1,2},{2,1},{3,4},{4,3},{5,6},{6,5},{7,8},{8,7},{9,10},{10... | collective-permute-start | bytes 2654216 | tf_op jit(solution)/shard_map/ppermute | solution.py:375
  90.1 2.0 %shard_map.80.refs_5_ = f32[384,1152]{1,0:T(8,128)S(1)} custom-call(f32[4]{0:T(128)S(1)} %pad_maximum_fusion.refs_0_.scalars, bf16[384,1152]{1,0:T(8,128)(2,1)S(1)} %get-tuple-element.65.refs_2_.refs_1_, bf16[384,1152]{1,0:T(8,128)(2,1)S(1)} %collective-permute-done.14.refs_2_, f32[384,1152]{1,0:T(8,128)S(1)} %shard_map.79.refs_3_), custom_call_target="tpu_custom_call", output_to_operand_aliasing={{}: (3, {})} | custom-call | flops 1 | bytes 1 | tf_op jit(solution)/shard_map/pallas_call | solution.py:267
  92.9 2.0 %shard_map.81.refs_3_ = f32[384,1152]{1,0:T(8,128)S(1)} custom-call(f32[4]{0:T(128)S(1)} %pad_maximum_fusion.refs_0_.scalars, bf16[384,1152]{1,0:T(8,128)(2,1)S(1)} %get-tuple-element.61.refs_1_.refs_2_, bf16[384,1152]{1,0:T(8,128)(2,1)S(1)} %collective-permute-done.12.refs_2_, f32[384,1152]{1,0:T(8,128)S(1)} %shard_map.78.refs_3_), custom_call_target="tpu_custom_call", output_to_operand_aliasing={{}: (3, {})} | custom-call | flops 1 | bytes 1 | tf_op jit(solution)/shard_map/pallas_call | solution.py:267
  94.9 2.7 %collective-permute-done.18 = f32[32,128]{1,0:T(8,128)S(1)} collective-permute-done((f32[32,128]{1,0:T(8,128)S(1)}, f32[32,128]{1,0:T(8,128)S(1)}, u32[]{:S(2)}, u32[]{:S(2)}) %collective-permute-start.18) | collective-permute-done | bytes 16416 | tf_op jit(solution)/shard_map/ppermute | solution.py:323
  97.6 4.6 %collective-permute-done.19 = f32[32,128]{1,0:T(8,128)S(1)} collective-permute-done((f32[32,128]{1,0:T(8,128)S(1)}, f32[32,128]{1,0:T(8,128)S(1)}, u32[]{:S(2)}, u32[]{:S(2)}) %collective-permute-start.19) | collective-permute-done | bytes 16416 | tf_op jit(solution)/shard_map/ppermute | solution.py:323
  102.3 2.0 %shard_map.82.refs_3_ = f32[384,1152]{1,0:T(8,128)S(1)} custom-call(f32[4]{0:T(128)S(1)} %pad_maximum_fusion.refs_0_.scalars, bf16[384,1152]{1,0:T(8,128)(2,1)S(1)} %get-tuple-element.61.refs_1_.refs_2_, bf16[384,1152]{1,0:T(8,128)(2,1)S(1)} %collective-permute-done.20.refs_2_, f32[384,1152]{1,0:T(8,128)S(1)} %shard_map.81.refs_3_), custom_call_target="tpu_custom_call", output_to_operand_aliasing={{}: (3, {})} | custom-call | flops 1 | bytes 1 | tf_op jit(solution)/shard_map/pallas_call | solution.py:267
  104.3 5.3 %collective-permute-start.21 = (f32[32,128]{1,0:T(8,128)S(1)}, f32[32,128]{1,0:T(8,128)S(1)}, u32[]{:S(2)}, u32[]{:S(2)}) collective-permute-start(f32[32,128]{1,0:T(8,128)S(1)} %add.54), channel_id=1, source_target_pairs={{0,8},{1,9},{2,10},{3,11},{4,12},{5,13},{6,14},{7,15},{8,0},{9,1},... | collective-permute-start | bytes 49160 | tf_op jit(solution)/shard_map/ppermute | solution.py:323
  109.6 5.3 %shard_map.83 = (f32[384,1152]{1,0:T(8,128)}, f32[384,1152]{1,0:T(8,128)}) custom-call(f32[4]{0:T(128)S(1)} %pad_maximum_fusion.refs_0_.scalars, bf16[384,1152]{1,0:T(8,128)(2,1)S(1)} %get-tuple-element.65.refs_2_.refs_1_, bf16[384,1152]{1,0:T(8,128)(2,1)S(1)} %collective-permute-done.5.refs_2_, bf16[192,1152]{1,0:T(8,128)(2,1)S(1)} %collective-permute-done.16.refs_3_, ...), custom_call_target="tpu_custom_call" | custom-call | flops 1 | bytes 1 | tf_op jit(solution)/shard_map/pallas_call | solution.py:267
  115.0 3.9 %shard_map.84 = (f32[384,1152]{1,0:T(8,128)}, f32[384,1152]{1,0:T(8,128)}) custom-call(f32[4]{0:T(128)S(1)} %pad_maximum_fusion.refs_0_.scalars, bf16[384,1152]{1,0:T(8,128)(2,1)S(1)} %get-tuple-element.61.refs_1_.refs_2_, bf16[384,1152]{1,0:T(8,128)(2,1)S(1)} %collective-permute-done.11.refs_2_, ...), custom_call_target="tpu_custom_call", output_to_operand_aliasing={{0}: (6, {}), {1}: (7, {})} | custom-call | flops 1 | bytes 1 | tf_op jit(solution)/shard_map/pallas_call | solution.py:267
  (57 shorter events, 17.7 us)
Async XLA Ops:
  2.4 9.7 %collective-permute-start.1 = (bf16[384,1152]{1,0:T(8,128)(2,1)S(1)}, bf16[384,1152]{1,0:T(8,128)(2,1)S(1)}, u32[]{:S(2)}, u32[]{:S(2)}) collective-permute-start(bf16[384,1152]{1,0:T(8,128)(2,1)S(1)} %get-tuple-element.65.refs_2_.refs_1_), channel_id=1, source_target_pairs={{0,1},{1,0},{2,3},{3,2},{4,5},{5,4},{6,7},{7,6},{8,9},{9,8},{10,11... | collective-permute-start | bytes 2654216 | tf_op jit(solution)/shard_map/ppermute | solution.py:320
  2.5 22.6 %collective-permute-start = (bf16[384,1152]{1,0:T(8,128)(2,1)S(1)}, bf16[384,1152]{1,0:T(8,128)(2,1)S(1)}, u32[]{:S(2)}, u32[]{:S(2)}) collective-permute-start(bf16[384,1152]{1,0:T(8,128)(2,1)S(1)} %get-tuple-element.61.refs_1_.refs_2_), channel_id=1, source_target_pairs={{0,254},{1,3},{2,0},{3,5},{4,2},{5,7},{6,4},{7,9},{8,6},{9,11},{10... | collective-permute-start | bytes 2654216 | tf_op jit(solution)/shard_map/ppermute | solution.py:314
  9.7 105.3 %copy-start = (f32[4]{0:T(128)}, f32[4]{0:T(128)S(1)}, u32[]{:S(2)}) copy-start(f32[4]{0:T(128)S(1)} %pad_maximum_fusion.refs_0_.scalars) | copy-start | bytes 52
  12.0 19.9 %collective-permute-start.4 = (bf16[384,1152]{1,0:T(8,128)(2,1)S(1)}, bf16[384,1152]{1,0:T(8,128)(2,1)S(1)}, u32[]{:S(2)}, u32[]{:S(2)}) collective-permute-start(bf16[384,1152]{1,0:T(8,128)(2,1)S(1)} %get-tuple-element.65.refs_2_.refs_1_), channel_id=1, source_target_pairs={{0,2},{1,255},{2,4},{3,1},{4,6},{5,3},{6,8},{7,5},{8,10},{9,7},{10... | collective-permute-start | bytes 2654216 | tf_op jit(solution)/shard_map/ppermute | solution.py:317
  25.1 22.5 %collective-permute-start.2 = (bf16[384,1152]{1,0:T(8,128)(2,1)S(1)}, bf16[384,1152]{1,0:T(8,128)(2,1)S(1)}, u32[]{:S(2)}, u32[]{:S(2)}) collective-permute-start(bf16[384,1152]{1,0:T(8,128)(2,1)S(1)} %collective-permute-done.refs_2_.refs_1_), channel_id=1, source_target_pairs={{0,254},{1,3},{2,0},{3,5},{4,2},{5,7},{6,4},{7,9},{8,6},{9,11},{10... | collective-permute-start | bytes 2654216 | tf_op jit(solution)/shard_map/ppermute | solution.py:314
  29.7 17.9 %collective-permute-start.3 = (bf16[384,1152]{1,0:T(8,128)(2,1)S(1)}, bf16[384,1152]{1,0:T(8,128)(2,1)S(1)}, u32[]{:S(2)}, u32[]{:S(2)}) collective-permute-start(bf16[384,1152]{1,0:T(8,128)(2,1)S(1)} %collective-permute-done.refs_2_.refs_1_), channel_id=1, source_target_pairs={{0,1},{1,0},{2,3},{3,2},{4,5},{5,4},{6,7},{7,6},{8,9},{9,8},{10,11... | collective-permute-start | bytes 2654216 | tf_op jit(solution)/shard_map/ppermute | solution.py:320
  31.9 24.0 %collective-permute-start.7 = (bf16[384,1152]{1,0:T(8,128)(2,1)S(1)}, bf16[384,1152]{1,0:T(8,128)(2,1)S(1)}, u32[]{:S(2)}, u32[]{:S(2)}) collective-permute-start(bf16[384,1152]{1,0:T(8,128)(2,1)S(1)} %collective-permute-done.4.refs_2_), channel_id=1, source_target_pairs={{0,2},{1,255},{2,4},{3,1},{4,6},{5,3},{6,8},{7,5},{8,10},{9,7},{10... | collective-permute-start | bytes 2654216 | tf_op jit(solution)/shard_map/ppermute | solution.py:317
  32.0 23.9 %collective-permute-start.8 = (bf16[384,1152]{1,0:T(8,128)(2,1)S(1)}, bf16[384,1152]{1,0:T(8,128)(2,1)S(1)}, u32[]{:S(2)}, u32[]{:S(2)}) collective-permute-start(bf16[384,1152]{1,0:T(8,128)(2,1)S(1)} %collective-permute-done.4.refs_2_), channel_id=1, source_target_pairs={{0,1},{1,0},{2,3},{3,2},{4,5},{5,4},{6,7},{7,6},{8,9},{9,8},{10,11... | collective-permute-start | bytes 2654216 | tf_op jit(solution)/shard_map/ppermute | solution.py:320
  47.6 10.8 %collective-permute-start.6 = (bf16[384,1152]{1,0:T(8,128)(2,1)S(1)}, bf16[384,1152]{1,0:T(8,128)(2,1)S(1)}, u32[]{:S(2)}, u32[]{:S(2)}) collective-permute-start(bf16[384,1152]{1,0:T(8,128)(2,1)S(1)} %collective-permute-done.2.refs_1_.refs_3_.refs_2_), channel_id=1, source_target_pairs={{0,1},{1,0},{2,3},{3,2},{4,5},{5,4},{6,7},{7,6},{8,9},{9,8},{10,11... | collective-permute-start | bytes 2654216 | tf_op jit(solution)/shard_map/ppermute | solution.py:320
  47.6 31.2 %collective-permute-start.5 = (bf16[384,1152]{1,0:T(8,128)(2,1)S(1)}, bf16[384,1152]{1,0:T(8,128)(2,1)S(1)}, u32[]{:S(2)}, u32[]{:S(2)}) collective-permute-start(bf16[384,1152]{1,0:T(8,128)(2,1)S(1)} %collective-permute-done.2.refs_1_.refs_3_.refs_2_), channel_id=1, source_target_pairs={{0,254},{1,3},{2,0},{3,5},{4,2},{5,7},{6,4},{7,9},{8,6},{9,11},{10... | collective-permute-start | bytes 2654216 | tf_op jit(solution)/shard_map/ppermute | solution.py:314
  55.9 34.2 %collective-permute-start.14 = (bf16[384,1152]{1,0:T(8,128)(2,1)S(1)}, bf16[384,1152]{1,0:T(8,128)(2,1)S(1)}, u32[]{:S(2)}, u32[]{:S(2)}) collective-permute-start(bf16[384,1152]{1,0:T(8,128)(2,1)S(1)} %collective-permute-done.7.refs_4_.refs_2_), channel_id=1, source_target_pairs={{0,1},{1,0},{2,3},{3,2},{4,5},{5,4},{6,7},{7,6},{8,9},{9,8},{10,11... | collective-permute-start | bytes 2654216 | tf_op jit(solution)/shard_map/ppermute | solution.py:320
  56.0 36.1 %collective-permute-start.12 = (bf16[384,1152]{1,0:T(8,128)(2,1)S(1)}, bf16[384,1152]{1,0:T(8,128)(2,1)S(1)}, u32[]{:S(2)}, u32[]{:S(2)}) collective-permute-start(bf16[384,1152]{1,0:T(8,128)(2,1)S(1)} %collective-permute-done.7.refs_4_.refs_2_), channel_id=1, source_target_pairs={{0,2},{1,255},{2,4},{3,1},{4,6},{5,3},{6,8},{7,5},{8,10},{9,7},{10... | collective-permute-start | bytes 2654216 | tf_op jit(solution)/shard_map/ppermute | solution.py:317
  61.1 10.9 %collective-permute-start.9 = (f32[32,128]{1,0:T(8,128)S(1)}, f32[32,128]{1,0:T(8,128)S(1)}, u32[]{:S(2)}, u32[]{:S(2)}) collective-permute-start(f32[32,128]{1,0:T(8,128)S(1)} %add_add_fusion), channel_id=1, source_target_pairs={{0,16},{1,17},{2,18},{3,19},{4,20},{5,21},{6,22},{7,23},{8,24},{9,... | collective-permute-start | bytes 49160 | tf_op jit(solution)/shard_map/ppermute | solution.py:323
  72.0 6.8 %collective-permute-start.10 = (f32[32,128]{1,0:T(8,128)S(1)}, f32[32,128]{1,0:T(8,128)S(1)}, u32[]{:S(2)}, u32[]{:S(2)}) collective-permute-start(f32[32,128]{1,0:T(8,128)S(1)} %add.49), channel_id=1, source_target_pairs={{0,32},{1,33},{2,34},{3,35},{4,36},{5,37},{6,38},{7,39},{8,40},{9,... | collective-permute-start | bytes 49160 | tf_op jit(solution)/shard_map/ppermute | solution.py:323
  78.8 3.8 %collective-permute-start.13 = (f32[32,128]{1,0:T(8,128)S(1)}, f32[32,128]{1,0:T(8,128)S(1)}, u32[]{:S(2)}, u32[]{:S(2)}) collective-permute-start(f32[32,128]{1,0:T(8,128)S(1)} %add.50), channel_id=1, source_target_pairs={{0,64},{1,65},{2,66},{3,67},{4,68},{5,69},{6,70},{7,71},{8,72},{9,... | collective-permute-start | bytes 49160 | tf_op jit(solution)/shard_map/ppermute | solution.py:323
  82.6 9.6 %collective-permute-start.15 = (f32[32,128]{1,0:T(8,128)S(1)}, f32[32,128]{1,0:T(8,128)S(1)}, u32[]{:S(2)}, u32[]{:S(2)}) collective-permute-start(f32[32,128]{1,0:T(8,128)S(1)} %add.51), channel_id=1, source_target_pairs={{0,128},{1,129},{2,130},{3,131},{4,132},{5,133},{6,134},{7,135},{8... | collective-permute-start | bytes 49160 | tf_op jit(solution)/shard_map/ppermute | solution.py:323
  84.1 18.2 %collective-permute-start.20 = (bf16[384,1152]{1,0:T(8,128)(2,1)S(1)}, bf16[384,1152]{1,0:T(8,128)(2,1)S(1)}, u32[]{:S(2)}, u32[]{:S(2)}) collective-permute-start(bf16[384,1152]{1,0:T(8,128)(2,1)S(1)} %collective-permute-done.5.refs_2_), channel_id=1, source_target_pairs={{0,1},{1,0},{2,3},{3,2},{4,5},{5,4},{6,7},{7,6},{8,9},{9,8},{10,11... | collective-permute-start | bytes 2654216 | tf_op jit(solution)/shard_map/ppermute | solution.py:320
  84.1 30.8 %collective-permute-start.11 = (bf16[384,1152]{1,0:T(8,128)(2,1)S(1)}, bf16[384,1152]{1,0:T(8,128)(2,1)S(1)}, u32[]{:S(2)}, u32[]{:S(2)}) collective-permute-start(bf16[384,1152]{1,0:T(8,128)(2,1)S(1)} %collective-permute-done.5.refs_2_), channel_id=1, source_target_pairs={{0,255},{1,2},{2,1},{3,4},{4,3},{5,6},{6,5},{7,8},{8,7},{9,10},{10... | collective-permute-start | bytes 2654216 | tf_op jit(solution)/shard_map/ppermute | solution.py:375
  92.3 17.4 %collective-permute-start.16 = (bf16[192,1152]{1,0:T(8,128)(2,1)S(1)}, bf16[192,1152]{1,0:T(8,128)(2,1)S(1)}, u32[]{:S(2)}, u32[]{:S(2)}) collective-permute-start(bf16[192,1152]{1,0:T(8,128)(2,1)S(1)} %get-tuple-element.120), channel_id=1, source_target_pairs={{0,1},{1,0},{2,3},{3,2},{4,5},{5,4},{6,7},{7,6},{8,9},{9,8},{10,11... | collective-permute-start | bytes 1327112 | tf_op jit(solution)/shard_map/ppermute | solution.py:320
  92.4 17.3 %collective-permute-start.17 = (bf16[192,1152]{1,0:T(8,128)(2,1)S(1)}, bf16[192,1152]{1,0:T(8,128)(2,1)S(1)}, u32[]{:S(2)}, u32[]{:S(2)}) collective-permute-start(bf16[192,1152]{1,0:T(8,128)(2,1)S(1)} %get-tuple-element.119), channel_id=1, source_target_pairs={{0,1},{1,0},{2,3},{3,2},{4,5},{5,4},{6,7},{7,6},{8,9},{9,8},{10,11... | collective-permute-start | bytes 1327112 | tf_op jit(solution)/shard_map/ppermute | solution.py:320
  92.9 4.7 %collective-permute-start.18 = (f32[32,128]{1,0:T(8,128)S(1)}, f32[32,128]{1,0:T(8,128)S(1)}, u32[]{:S(2)}, u32[]{:S(2)}) collective-permute-start(f32[32,128]{1,0:T(8,128)S(1)} %add.52), channel_id=1, source_target_pairs={{0,2},{1,3},{2,0},{3,1},{4,6},{5,7},{6,4},{7,5},{8,10},{9,11},{10,... | collective-permute-start | bytes 49160 | tf_op jit(solution)/shard_map/ppermute | solution.py:323
  97.6 4.6 %collective-permute-start.19 = (f32[32,128]{1,0:T(8,128)S(1)}, f32[32,128]{1,0:T(8,128)S(1)}, u32[]{:S(2)}, u32[]{:S(2)}) collective-permute-start(f32[32,128]{1,0:T(8,128)S(1)} %add.53), channel_id=1, source_target_pairs={{0,4},{1,5},{2,6},{3,7},{4,0},{5,1},{6,2},{7,3},{8,12},{9,13},{10,... | collective-permute-start | bytes 49160 | tf_op jit(solution)/shard_map/ppermute | solution.py:323
  104.3 10.6 %collective-permute-start.21 = (f32[32,128]{1,0:T(8,128)S(1)}, f32[32,128]{1,0:T(8,128)S(1)}, u32[]{:S(2)}, u32[]{:S(2)}) collective-permute-start(f32[32,128]{1,0:T(8,128)S(1)} %add.54), channel_id=1, source_target_pairs={{0,8},{1,9},{2,10},{3,11},{4,12},{5,13},{6,14},{7,15},{8,0},{9,1},... | collective-permute-start | bytes 49160 | tf_op jit(solution)/shard_map/ppermute | solution.py:323
  114.9 4.0 %collective-permute-start.22 = (f32[32,128]{1,0:T(8,128)S(1)}, f32[32,128]{1,0:T(8,128)S(1)}, u32[]{:S(2)}, u32[]{:S(2)}) collective-permute-start(f32[32,128]{1,0:T(8,128)S(1)} %add.55.mine), channel_id=1, source_target_pairs={{0,1},{1,0},{2,3},{3,2},{4,5},{5,4},{6,7},{7,6},{8,9},{9,8},{10,11... | collective-permute-start | bytes 49160 | tf_op jit(solution)/shard_map/ppermute | solution.py:323
  (2 other events, 4.7 us)

commit v3 on v2

--- a/solution.py
+++ b/solution.py
@@ -333,9 +333,9 @@
     p1 = up(a)
     sibling = swap(b)
     acc_a, stats0 = stage(scalars, a, [b], ["all"], label=True)
-    b, acc_a = tied(b, acc_a)
+    acc_b, stats1 = stage(scalars, b, [a, sibling], [None, "core1"], label=True)
+    b, acc_a, acc_b = tied(b, acc_a, acc_b)
     r1 = down(b)
-    acc_b, stats1 = stage(scalars, b, [a, sibling], [None, "core1"], label=True)
 
     p1, acc_a, acc_b = tied(p1, acc_a, acc_b)
     p2, from_p1 = up(p1), swap(p1)
@@ -375,7 +375,7 @@
     last, from_p3 = lax.ppermute(p3, "dp", cross), swap(p3)
     stats = all_added(stats, next(rounds))
     (acc_b,) = stage(scalars, b, [p2], [None], acc_b)
-    stats, acc_a, acc_b = tied(stats, acc_a, acc_b)
+    from_r2, stats, acc_a, acc_b = tied(from_r2, stats, acc_a, acc_b)
     stats = all_added(stats, next(rounds))
     (acc_b,) = stage(scalars, b, [from_r2], [None], acc_b)
 
@@ -383,10 +383,10 @@
     from_r3 = [swap(r3[:half]), swap(r3[half:])]
     stats = all_added(stats, next(rounds))
     (acc_a,) = stage(scalars, a, [r3], [None], acc_a)
-    stats, acc_a, acc_b = tied(stats, acc_a, acc_b)
+    from_p3, stats, acc_a, acc_b = tied(from_p3, stats, acc_a, acc_b)
     stats = all_added(stats, next(rounds))
     (acc_a,) = stage(scalars, a, [from_p3], [None], acc_a)
-    stats, acc_a, acc_b = tied(stats, acc_a, acc_b)
+    *from_r3, stats, acc_a, acc_b = tied(*from_r3, stats, acc_a, acc_b)
     stats = all_added(stats, next(rounds))
     outs = stage(
         scalars, b, [p3, *from_r3], [None, None, None], acc_b, final=(1, x, y, None)

time: 123 us -> 119 us (0.967)
  waiting for transfers between devices: 38.1 us -> 34.5 us
    ppermute x3, waiting for transfers between devices: 21.8 us -> 10.5 us  [up(): return lax.ppermute(value, 'dp', up_down)]
    ppermute x3, waiting for transfers between devices: 0.01 us -> 10.2 us  [down(): return lax.ppermute(value, 'dp', down_up)]
    ppermute x8, waiting for transfers between devices: 16.2 us -> 13.8 us  [exchanged(): return lax.ppermute(value, 'dp', [(d, d ^ distance) for d in range(count)])]
  transfers between devices with their start and end apart: 23 -> 23, of which waited for: 6 -> 8; matrix products, arithmetic and copies ran while one was open for 0% -> 0% of each run, Pallas kernels for 33% -> 35%
where the time goes in v3:
time: 119 us; the launch traced here: 117 us
  Pallas kernels  43.7 us (37%)
  starting transfers between devices  36 us (30%)
  waiting for transfers between devices  34.5 us (29%)
  between operations  2.52 us (2%)
    pallas_call x14, Pallas kernels, stage(): pl.pallas_call(functools.partial(stage_kernel, plan), out_shape=out_shape...  34.8 us
    ppermute x3, starting transfers between devices, up(): return lax.ppermute(value, 'dp', up_down)  15 us
    ppermute x8, starting transfers between devices, exchanged(): return lax.ppermute(value, 'dp', [(d, d ^ distance) for d in range(count)])  14.1 us
    ppermute x8, waiting for transfers between devices, exchanged(): return lax.ppermute(value, 'dp', [(d, d ^ distance) for d in range(count)])  13.8 us
    ppermute x3, waiting for transfers between devices, up(): return lax.ppermute(value, 'dp', up_down)  10.5 us
    ppermute x3, waiting for transfers between devices, down(): return lax.ppermute(value, 'dp', down_up)  10.2 us
    ppermute x1, starting transfers between devices, per_device(): last, from_p3 = (lax.ppermute(p3, 'dp', cross), swap(p3))  6.09 us
    pallas_call x3, Pallas kernels, middle(): pl.pallas_call(functools.partial(middle_kernel, plan), out_shape=jax.Shap...  5.74 us
  transfers between devices with their start and end apart: 23, of which 8 were waited for; matrix products, arithmetic and copies ran while one was open for 0% of the time, Pallas kernels for 35%

profile of v3, /device:TPU:16, one launch (start us, length us, event | category | flops | bytes accessed | tf_op | source)
XLA Modules:
  0.0 117.5 jit_solution(149437417789551528)
XLA Ops:
  2.5 5.8 %collective-permute-start = (bf16[384,1152]{1,0:T(8,128)(2,1)S(1)}, bf16[384,1152]{1,0:T(8,128)(2,1)S(1)}, u32[]{:S(2)}, u32[]{:S(2)}) collective-permute-start(bf16[384,1152]{1,0:T(8,128)(2,1)S(1)} %get-tuple-element.66.refs_1_.refs_2_), channel_id=1, source_target_pairs={{0,254},{1,3},{2,0},{3,5},{4,2},{5,7},{6,4},{7,9},{8,6},{9,11},{10... | collective-permute-start | bytes 2654216 | tf_op jit(solution)/shard_map/ppermute | solution.py:314
  9.7 2.2 %shard_map.68 = (f32[384,1152]{1,0:T(8,128)S(1)}, f32[32,128]{1,0:T(8,128)S(1)}) custom-call(f32[4]{0:T(128)S(1)} %pad_maximum_fusion.refs_0_.scalars, bf16[384,1152]{1,0:T(8,128)(2,1)S(1)} %get-tuple-element.66.refs_1_.refs_2_, bf16[384,1152]{1,0:T(8,128)(2,1)S(1)} %get-tuple-element.73.refs_2_.refs_1_), custom_call_target="tpu_custom_call" | custom-call | flops 1 | bytes 1 | tf_op jit(solution)/shard_map/pallas_call | solution.py:267
  12.0 2.6 %shard_map.69 = (f32[384,1152]{1,0:T(8,128)S(1)}, f32[32,128]{1,0:T(8,128)S(1)}) custom-call(f32[4]{0:T(128)S(1)} %pad_maximum_fusion.refs_0_.scalars, bf16[384,1152]{1,0:T(8,128)(2,1)S(1)} %get-tuple-element.73.refs_2_.refs_1_, bf16[384,1152]{1,0:T(8,128)(2,1)S(1)} %get-tuple-element.66.refs_1_.refs_2_, bf16[384,1152]{1,0:T(8,128)(2,1)S(1)} %collective-permute-done.1.refs_3_), custom_call_target="tpu_custom_call" | custom-call | flops 1 | bytes 1 | tf_op jit(solution)/shard_map/pallas_call | solution.py:267
  14.7 7.8 %collective-permute-done.refs_2_.refs_1_ = bf16[384,1152]{1,0:T(8,128)(2,1)S(1)} collective-permute-done((bf16[384,1152]{1,0:T(8,128)(2,1)S(1)}, bf16[384,1152]{1,0:T(8,128)(2,1)S(1)}, u32[]{:S(2)}, u32[]{:S(2)}) %collective-permute-start) | collective-permute-done | bytes 884768 | tf_op jit(solution)/shard_map/ppermute | solution.py:314
  22.5 4.6 %collective-permute-start.2 = (bf16[384,1152]{1,0:T(8,128)(2,1)S(1)}, bf16[384,1152]{1,0:T(8,128)(2,1)S(1)}, u32[]{:S(2)}, u32[]{:S(2)}) collective-permute-start(bf16[384,1152]{1,0:T(8,128)(2,1)S(1)} %collective-permute-done.refs_2_.refs_1_), channel_id=1, source_target_pairs={{0,254},{1,3},{2,0},{3,5},{4,2},{5,7},{6,4},{7,9},{8,6},{9,11},{10... | collective-permute-start | bytes 2654216 | tf_op jit(solution)/shard_map/ppermute | solution.py:314
  27.1 2.2 %shard_map.70 = (f32[384,1152]{1,0:T(8,128)S(1)}, f32[32,128]{1,0:T(8,128)S(1)}) custom-call(f32[4]{0:T(128)S(1)} %pad_maximum_fusion.refs_0_.scalars, bf16[384,1152]{1,0:T(8,128)(2,1)S(1)} %get-tuple-element.73.refs_2_.refs_1_, bf16[384,1152]{1,0:T(8,128)(2,1)S(1)} %collective-permute-done.refs_2_.refs_1_, ...), custom_call_target="tpu_custom_call", output_to_operand_aliasing={{0}: (3, {})} | custom-call | flops 1 | bytes 1 | tf_op jit(solution)/shard_map/pallas_call | solution.py:267
  29.3 6.8 %collective-permute-done.4.refs_2_ = bf16[384,1152]{1,0:T(8,128)(2,1)S(1)} collective-permute-done((bf16[384,1152]{1,0:T(8,128)(2,1)S(1)}, bf16[384,1152]{1,0:T(8,128)(2,1)S(1)}, u32[]{:S(2)}, u32[]{:S(2)}) %collective-permute-start.4) | collective-permute-done | bytes 884768 | tf_op jit(solution)/shard_map/ppermute | solution.py:317
  37.6 2.0 %shard_map.71.refs_3_ = f32[384,1152]{1,0:T(8,128)S(1)} custom-call(f32[4]{0:T(128)S(1)} %pad_maximum_fusion.refs_0_.scalars, bf16[384,1152]{1,0:T(8,128)(2,1)S(1)} %get-tuple-element.66.refs_1_.refs_2_, bf16[384,1152]{1,0:T(8,128)(2,1)S(1)} %collective-permute-done.4.refs_2_, f32[384,1152]{1,0:T(8,128)S(1)} %get-tuple-element.77.refs_3_), custom_call_target="tpu_custom_call", output_to_operand_aliasing={{}: (3, {})} | custom-call | flops 1 | bytes 1 | tf_op jit(solution)/shard_map/pallas_call | solution.py:267
  39.6 2.7 %collective-permute-done.2.refs_1_.refs_3_.refs_2_ = bf16[384,1152]{1,0:T(8,128)(2,1)S(1)} collective-permute-done((bf16[384,1152]{1,0:T(8,128)(2,1)S(1)}, bf16[384,1152]{1,0:T(8,128)(2,1)S(1)}, u32[]{:S(2)}, u32[]{:S(2)}) %collective-permute-start.2) | collective-permute-done | bytes 884768 | tf_op jit(solution)/shard_map/ppermute | solution.py:314
  42.3 4.6 %collective-permute-start.5 = (bf16[384,1152]{1,0:T(8,128)(2,1)S(1)}, bf16[384,1152]{1,0:T(8,128)(2,1)S(1)}, u32[]{:S(2)}, u32[]{:S(2)}) collective-permute-start(bf16[384,1152]{1,0:T(8,128)(2,1)S(1)} %collective-permute-done.2.refs_1_.refs_3_.refs_2_), channel_id=1, source_target_pairs={{0,254},{1,3},{2,0},{3,5},{4,2},{5,7},{6,4},{7,9},{8,6},{9,11},{10... | collective-permute-start | bytes 2654216 | tf_op jit(solution)/shard_map/ppermute | solution.py:314
  48.4 2.2 %shard_map.73 = (f32[384,1152]{1,0:T(8,128)S(1)}, f32[32,128]{1,0:T(8,128)S(1)}) custom-call(f32[4]{0:T(128)S(1)} %pad_maximum_fusion.refs_0_.scalars, bf16[384,1152]{1,0:T(8,128)(2,1)S(1)} %get-tuple-element.66.refs_1_.refs_2_, bf16[384,1152]{1,0:T(8,128)(2,1)S(1)} %collective-permute-done.3.refs_2_.refs_5_, ...), custom_call_target="tpu_custom_call", output_to_operand_aliasing={{0}: (3, {})} | custom-call | flops 1 | bytes 1 | tf_op jit(solution)/shard_map/pallas_call | solution.py:267
  50.6 3.4 %collective-permute-done.7.refs_4_.refs_2_ = bf16[384,1152]{1,0:T(8,128)(2,1)S(1)} collective-permute-done((bf16[384,1152]{1,0:T(8,128)(2,1)S(1)}, bf16[384,1152]{1,0:T(8,128)(2,1)S(1)}, u32[]{:S(2)}, u32[]{:S(2)}) %collective-permute-start.7) | collective-permute-done | bytes 884768 | tf_op jit(solution)/shard_map/ppermute | solution.py:317
  54.1 2.2 %shard_map.75 = (f32[384,1152]{1,0:T(8,128)S(1)}, f32[32,128]{1,0:T(8,128)S(1)}) custom-call(f32[4]{0:T(128)S(1)} %pad_maximum_fusion.refs_0_.scalars, bf16[384,1152]{1,0:T(8,128)(2,1)S(1)} %get-tuple-element.73.refs_2_.refs_1_, bf16[384,1152]{1,0:T(8,128)(2,1)S(1)} %collective-permute-done.8.refs_2_.refs_6_, ...), custom_call_target="tpu_custom_call", output_to_operand_aliasing={{0}: (3, {})} | custom-call | flops 1 | bytes 1 | tf_op jit(solution)/shard_map/pallas_call | solution.py:267
  56.3 2.7 %shard_map.76 = f32[32,128]{1,0:T(8,128)S(1)} custom-call(f32[4]{0:T(128)S(1)} %pad_maximum_fusion.refs_0_.scalars, bf16[384,1152]{1,0:T(8,128)(2,1)S(1)} %collective-permute-done.refs_2_.refs_1_, bf16[384,1152]{1,0:T(8,128)(2,1)S(1)} %collective-permute-done.4.refs_2_, bf16[384,1152]{1,0:T(8,128)(2,1)S(1)} %collective-permute-done.2.refs_1_.refs_3_.refs_2_, ...), custom_call_target="tpu_custom_call" | custom-call | flops 1 | bytes 1 | tf_op jit(solution)/shard_map/pallas_call | solution.py:223
  60.7 2.0 %shard_map.77.refs_3_ = f32[384,1152]{1,0:T(8,128)S(1)} custom-call(f32[4]{0:T(128)S(1)} %pad_maximum_fusion.refs_0_.scalars, bf16[384,1152]{1,0:T(8,128)(2,1)S(1)} %get-tuple-element.66.refs_1_.refs_2_, bf16[384,1152]{1,0:T(8,128)(2,1)S(1)} %collective-permute-done.7.refs_4_.refs_2_, ...), custom_call_target="tpu_custom_call", output_to_operand_aliasing={{}: (3, {})} | custom-call | flops 1 | bytes 1 | tf_op jit(solution)/shard_map/pallas_call | solution.py:267
  62.8 6.9 %collective-permute-done.9 = f32[32,128]{1,0:T(8,128)S(1)} collective-permute-done((f32[32,128]{1,0:T(8,128)S(1)}, f32[32,128]{1,0:T(8,128)S(1)}, u32[]{:S(2)}, u32[]{:S(2)}) %collective-permute-start.9) | collective-permute-done | bytes 16416 | tf_op jit(solution)/shard_map/ppermute | solution.py:323
  69.6 5.0 %collective-permute-start.10 = (f32[32,128]{1,0:T(8,128)S(1)}, f32[32,128]{1,0:T(8,128)S(1)}, u32[]{:S(2)}, u32[]{:S(2)}) collective-permute-start(f32[32,128]{1,0:T(8,128)S(1)} %add.49), channel_id=1, source_target_pairs={{0,32},{1,33},{2,34},{3,35},{4,36},{5,37},{6,38},{7,39},{8,40},{9,... | collective-permute-start | bytes 49160 | tf_op jit(solution)/shard_map/ppermute | solution.py:323
  81.8 6.1 %collective-permute-start.11 = (bf16[384,1152]{1,0:T(8,128)(2,1)S(1)}, bf16[384,1152]{1,0:T(8,128)(2,1)S(1)}, u32[]{:S(2)}, u32[]{:S(2)}) collective-permute-start(bf16[384,1152]{1,0:T(8,128)(2,1)S(1)} %collective-permute-done.5.refs_2_), channel_id=1, source_target_pairs={{0,255},{1,2},{2,1},{3,4},{4,3},{5,6},{6,5},{7,8},{8,7},{9,10},{10... | collective-permute-start | bytes 2654216 | tf_op jit(solution)/shard_map/ppermute | solution.py:375
  87.9 2.0 %shard_map.80.refs_5_ = f32[384,1152]{1,0:T(8,128)S(1)} custom-call(f32[4]{0:T(128)S(1)} %pad_maximum_fusion.refs_0_.scalars, bf16[384,1152]{1,0:T(8,128)(2,1)S(1)} %get-tuple-element.73.refs_2_.refs_1_, bf16[384,1152]{1,0:T(8,128)(2,1)S(1)} %collective-permute-done.13.refs_2_, f32[384,1152]{1,0:T(8,128)S(1)} %shard_map.79.refs_3_), custom_call_target="tpu_custom_call", output_to_operand_aliasing={{}: (3, {})} | custom-call | flops 1 | bytes 1 | tf_op jit(solution)/shard_map/pallas_call | solution.py:267
  92.7 2.6 %collective-permute-done.19 = f32[32,128]{1,0:T(8,128)S(1)} collective-permute-done((f32[32,128]{1,0:T(8,128)S(1)}, f32[32,128]{1,0:T(8,128)S(1)}, u32[]{:S(2)}, u32[]{:S(2)}) %collective-permute-start.19) | collective-permute-done | bytes 16416 | tf_op jit(solution)/shard_map/ppermute | solution.py:323
  97.5 2.6 %collective-permute-done.20 = f32[32,128]{1,0:T(8,128)S(1)} collective-permute-done((f32[32,128]{1,0:T(8,128)S(1)}, f32[32,128]{1,0:T(8,128)S(1)}, u32[]{:S(2)}, u32[]{:S(2)}) %collective-permute-start.20) | collective-permute-done | bytes 16416 | tf_op jit(solution)/shard_map/ppermute | solution.py:323
  100.1 5.8 %collective-permute-start.21 = (f32[32,128]{1,0:T(8,128)S(1)}, f32[32,128]{1,0:T(8,128)S(1)}, u32[]{:S(2)}, u32[]{:S(2)}) collective-permute-start(f32[32,128]{1,0:T(8,128)S(1)} %add.54), channel_id=1, source_target_pairs={{0,8},{1,9},{2,10},{3,11},{4,12},{5,13},{6,14},{7,15},{8,0},{9,1},... | collective-permute-start | bytes 49160 | tf_op jit(solution)/shard_map/ppermute | solution.py:323
  105.9 5.2 %shard_map.83 = (f32[384,1152]{1,0:T(8,128)}, f32[384,1152]{1,0:T(8,128)}) custom-call(f32[4]{0:T(128)S(1)} %pad_maximum_fusion.refs_0_.scalars, bf16[384,1152]{1,0:T(8,128)(2,1)S(1)} %get-tuple-element.73.refs_2_.refs_1_, bf16[384,1152]{1,0:T(8,128)(2,1)S(1)} %collective-permute-done.5.refs_2_, bf16[192,1152]{1,0:T(8,128)(2,1)S(1)} %collective-permute-done.16.refs_3_, ...), custom_call_target="tpu_custom_call" | custom-call | flops 1 | bytes 1 | tf_op jit(solution)/shard_map/pallas_call | solution.py:267
  111.4 3.9 %shard_map.84 = (f32[384,1152]{1,0:T(8,128)}, f32[384,1152]{1,0:T(8,128)}) custom-call(f32[4]{0:T(128)S(1)} %pad_maximum_fusion.refs_0_.scalars, bf16[384,1152]{1,0:T(8,128)(2,1)S(1)} %get-tuple-element.66.refs_1_.refs_2_, bf16[384,1152]{1,0:T(8,128)(2,1)S(1)} %collective-permute-done.11.refs_2_, ...), custom_call_target="tpu_custom_call", output_to_operand_aliasing={{0}: (6, {}), {1}: (7, {})} | custom-call | flops 1 | bytes 1 | tf_op jit(solution)/shard_map/pallas_call | solution.py:267
  (57 shorter events, 20.8 us)
Async XLA Ops:
  2.4 9.6 %collective-permute-start.1 = (bf16[384,1152]{1,0:T(8,128)(2,1)S(1)}, bf16[384,1152]{1,0:T(8,128)(2,1)S(1)}, u32[]{:S(2)}, u32[]{:S(2)}) collective-permute-start(bf16[384,1152]{1,0:T(8,128)(2,1)S(1)} %get-tuple-element.73.refs_2_.refs_1_), channel_id=1, source_target_pairs={{0,1},{1,0},{2,3},{3,2},{4,5},{5,4},{6,7},{7,6},{8,9},{9,8},{10,11... | collective-permute-start | bytes 2654216 | tf_op jit(solution)/shard_map/ppermute | solution.py:320
  2.5 20.0 %collective-permute-start = (bf16[384,1152]{1,0:T(8,128)(2,1)S(1)}, bf16[384,1152]{1,0:T(8,128)(2,1)S(1)}, u32[]{:S(2)}, u32[]{:S(2)}) collective-permute-start(bf16[384,1152]{1,0:T(8,128)(2,1)S(1)} %get-tuple-element.66.refs_1_.refs_2_), channel_id=1, source_target_pairs={{0,254},{1,3},{2,0},{3,5},{4,2},{5,7},{6,4},{7,9},{8,6},{9,11},{10... | collective-permute-start | bytes 2654216 | tf_op jit(solution)/shard_map/ppermute | solution.py:314
  9.7 101.6 %copy-start = (f32[4]{0:T(128)}, f32[4]{0:T(128)S(1)}, u32[]{:S(2)}) copy-start(f32[4]{0:T(128)S(1)} %pad_maximum_fusion.refs_0_.scalars) | copy-start | bytes 52
  14.6 21.4 %collective-permute-start.4 = (bf16[384,1152]{1,0:T(8,128)(2,1)S(1)}, bf16[384,1152]{1,0:T(8,128)(2,1)S(1)}, u32[]{:S(2)}, u32[]{:S(2)}) collective-permute-start(bf16[384,1152]{1,0:T(8,128)(2,1)S(1)} %get-tuple-element.73.refs_2_.refs_1_), channel_id=1, source_target_pairs={{0,2},{1,255},{2,4},{3,1},{4,6},{5,3},{6,8},{7,5},{8,10},{9,7},{10... | collective-permute-start | bytes 2654216 | tf_op jit(solution)/shard_map/ppermute | solution.py:317
  22.5 19.8 %collective-permute-start.2 = (bf16[384,1152]{1,0:T(8,128)(2,1)S(1)}, bf16[384,1152]{1,0:T(8,128)(2,1)S(1)}, u32[]{:S(2)}, u32[]{:S(2)}) collective-permute-start(bf16[384,1152]{1,0:T(8,128)(2,1)S(1)} %collective-permute-done.refs_2_.refs_1_), channel_id=1, source_target_pairs={{0,254},{1,3},{2,0},{3,5},{4,2},{5,7},{6,4},{7,9},{8,6},{9,11},{10... | collective-permute-start | bytes 2654216 | tf_op jit(solution)/shard_map/ppermute | solution.py:314
  27.1 15.2 %collective-permute-start.3 = (bf16[384,1152]{1,0:T(8,128)(2,1)S(1)}, bf16[384,1152]{1,0:T(8,128)(2,1)S(1)}, u32[]{:S(2)}, u32[]{:S(2)}) collective-permute-start(bf16[384,1152]{1,0:T(8,128)(2,1)S(1)} %collective-permute-done.refs_2_.refs_1_), channel_id=1, source_target_pairs={{0,1},{1,0},{2,3},{3,2},{4,5},{5,4},{6,7},{7,6},{8,9},{9,8},{10,11... | collective-permute-start | bytes 2654216 | tf_op jit(solution)/shard_map/ppermute | solution.py:320
  36.0 18.0 %collective-permute-start.7 = (bf16[384,1152]{1,0:T(8,128)(2,1)S(1)}, bf16[384,1152]{1,0:T(8,128)(2,1)S(1)}, u32[]{:S(2)}, u32[]{:S(2)}) collective-permute-start(bf16[384,1152]{1,0:T(8,128)(2,1)S(1)} %collective-permute-done.4.refs_2_), channel_id=1, source_target_pairs={{0,2},{1,255},{2,4},{3,1},{4,6},{5,3},{6,8},{7,5},{8,10},{9,7},{10... | collective-permute-start | bytes 2654216 | tf_op jit(solution)/shard_map/ppermute | solution.py:317
  36.0 18.0 %collective-permute-start.8 = (bf16[384,1152]{1,0:T(8,128)(2,1)S(1)}, bf16[384,1152]{1,0:T(8,128)(2,1)S(1)}, u32[]{:S(2)}, u32[]{:S(2)}) collective-permute-start(bf16[384,1152]{1,0:T(8,128)(2,1)S(1)} %collective-permute-done.4.refs_2_), channel_id=1, source_target_pairs={{0,1},{1,0},{2,3},{3,2},{4,5},{5,4},{6,7},{7,6},{8,9},{9,8},{10,11... | collective-permute-start | bytes 2654216 | tf_op jit(solution)/shard_map/ppermute | solution.py:320
  42.3 14.0 %collective-permute-start.6 = (bf16[384,1152]{1,0:T(8,128)(2,1)S(1)}, bf16[384,1152]{1,0:T(8,128)(2,1)S(1)}, u32[]{:S(2)}, u32[]{:S(2)}) collective-permute-start(bf16[384,1152]{1,0:T(8,128)(2,1)S(1)} %collective-permute-done.2.refs_1_.refs_3_.refs_2_), channel_id=1, source_target_pairs={{0,1},{1,0},{2,3},{3,2},{4,5},{5,4},{6,7},{7,6},{8,9},{9,8},{10,11... | collective-permute-start | bytes 2654216 | tf_op jit(solution)/shard_map/ppermute | solution.py:320
  42.3 34.4 %collective-permute-start.5 = (bf16[384,1152]{1,0:T(8,128)(2,1)S(1)}, bf16[384,1152]{1,0:T(8,128)(2,1)S(1)}, u32[]{:S(2)}, u32[]{:S(2)}) collective-permute-start(bf16[384,1152]{1,0:T(8,128)(2,1)S(1)} %collective-permute-done.2.refs_1_.refs_3_.refs_2_), channel_id=1, source_target_pairs={{0,254},{1,3},{2,0},{3,5},{4,2},{5,7},{6,4},{7,9},{8,6},{9,11},{10... | collective-permute-start | bytes 2654216 | tf_op jit(solution)/shard_map/ppermute | solution.py:314
  54.1 26.5 %collective-permute-start.13 = (bf16[384,1152]{1,0:T(8,128)(2,1)S(1)}, bf16[384,1152]{1,0:T(8,128)(2,1)S(1)}, u32[]{:S(2)}, u32[]{:S(2)}) collective-permute-start(bf16[384,1152]{1,0:T(8,128)(2,1)S(1)} %collective-permute-done.7.refs_4_.refs_2_), channel_id=1, source_target_pairs={{0,1},{1,0},{2,3},{3,2},{4,5},{5,4},{6,7},{7,6},{8,9},{9,8},{10,11... | collective-permute-start | bytes 2654216 | tf_op jit(solution)/shard_map/ppermute | solution.py:320
  54.1 35.9 %collective-permute-start.12 = (bf16[384,1152]{1,0:T(8,128)(2,1)S(1)}, bf16[384,1152]{1,0:T(8,128)(2,1)S(1)}, u32[]{:S(2)}, u32[]{:S(2)}) collective-permute-start(bf16[384,1152]{1,0:T(8,128)(2,1)S(1)} %collective-permute-done.7.refs_4_.refs_2_), channel_id=1, source_target_pairs={{0,2},{1,255},{2,4},{3,1},{4,6},{5,3},{6,8},{7,5},{8,10},{9,7},{10... | collective-permute-start | bytes 2654216 | tf_op jit(solution)/shard_map/ppermute | solution.py:317
  59.1 10.6 %collective-permute-start.9 = (f32[32,128]{1,0:T(8,128)S(1)}, f32[32,128]{1,0:T(8,128)S(1)}, u32[]{:S(2)}, u32[]{:S(2)}) collective-permute-start(f32[32,128]{1,0:T(8,128)S(1)} %add_add_fusion), channel_id=1, source_target_pairs={{0,16},{1,17},{2,18},{3,19},{4,20},{5,21},{6,22},{7,23},{8,24},{9,... | collective-permute-start | bytes 49160 | tf_op jit(solution)/shard_map/ppermute | solution.py:323
  69.6 7.0 %collective-permute-start.10 = (f32[32,128]{1,0:T(8,128)S(1)}, f32[32,128]{1,0:T(8,128)S(1)}, u32[]{:S(2)}, u32[]{:S(2)}) collective-permute-start(f32[32,128]{1,0:T(8,128)S(1)} %add.49), channel_id=1, source_target_pairs={{0,32},{1,33},{2,34},{3,35},{4,36},{5,37},{6,38},{7,39},{8,40},{9,... | collective-permute-start | bytes 49160 | tf_op jit(solution)/shard_map/ppermute | solution.py:323
  76.7 3.8 %collective-permute-start.14 = (f32[32,128]{1,0:T(8,128)S(1)}, f32[32,128]{1,0:T(8,128)S(1)}, u32[]{:S(2)}, u32[]{:S(2)}) collective-permute-start(f32[32,128]{1,0:T(8,128)S(1)} %add.50), channel_id=1, source_target_pairs={{0,64},{1,65},{2,66},{3,67},{4,68},{5,69},{6,70},{7,71},{8,72},{9,... | collective-permute-start | bytes 49160 | tf_op jit(solution)/shard_map/ppermute | solution.py:323
  80.5 9.4 %collective-permute-start.15 = (f32[32,128]{1,0:T(8,128)S(1)}, f32[32,128]{1,0:T(8,128)S(1)}, u32[]{:S(2)}, u32[]{:S(2)}) collective-permute-start(f32[32,128]{1,0:T(8,128)S(1)} %add.51), channel_id=1, source_target_pairs={{0,128},{1,129},{2,130},{3,131},{4,132},{5,133},{6,134},{7,135},{8... | collective-permute-start | bytes 49160 | tf_op jit(solution)/shard_map/ppermute | solution.py:323
  81.8 13.5 %collective-permute-start.18 = (bf16[384,1152]{1,0:T(8,128)(2,1)S(1)}, bf16[384,1152]{1,0:T(8,128)(2,1)S(1)}, u32[]{:S(2)}, u32[]{:S(2)}) collective-permute-start(bf16[384,1152]{1,0:T(8,128)(2,1)S(1)} %collective-permute-done.5.refs_2_), channel_id=1, source_target_pairs={{0,1},{1,0},{2,3},{3,2},{4,5},{5,4},{6,7},{7,6},{8,9},{9,8},{10,11... | collective-permute-start | bytes 2654216 | tf_op jit(solution)/shard_map/ppermute | solution.py:320
  81.8 29.4 %collective-permute-start.11 = (bf16[384,1152]{1,0:T(8,128)(2,1)S(1)}, bf16[384,1152]{1,0:T(8,128)(2,1)S(1)}, u32[]{:S(2)}, u32[]{:S(2)}) collective-permute-start(bf16[384,1152]{1,0:T(8,128)(2,1)S(1)} %collective-permute-done.5.refs_2_), channel_id=1, source_target_pairs={{0,255},{1,2},{2,1},{3,4},{4,3},{5,6},{6,5},{7,8},{8,7},{9,10},{10... | collective-permute-start | bytes 2654216 | tf_op jit(solution)/shard_map/ppermute | solution.py:375
  90.1 10.0 %collective-permute-start.16 = (bf16[192,1152]{1,0:T(8,128)(2,1)S(1)}, bf16[192,1152]{1,0:T(8,128)(2,1)S(1)}, u32[]{:S(2)}, u32[]{:S(2)}) collective-permute-start(bf16[192,1152]{1,0:T(8,128)(2,1)S(1)} %get-tuple-element.130), channel_id=1, source_target_pairs={{0,1},{1,0},{2,3},{3,2},{4,5},{5,4},{6,7},{7,6},{8,9},{9,8},{10,11... | collective-permute-start | bytes 1327112 | tf_op jit(solution)/shard_map/ppermute | solution.py:320
  90.2 9.9 %collective-permute-start.17 = (bf16[192,1152]{1,0:T(8,128)(2,1)S(1)}, bf16[192,1152]{1,0:T(8,128)(2,1)S(1)}, u32[]{:S(2)}, u32[]{:S(2)}) collective-permute-start(bf16[192,1152]{1,0:T(8,128)(2,1)S(1)} %get-tuple-element.129), channel_id=1, source_target_pairs={{0,1},{1,0},{2,3},{3,2},{4,5},{5,4},{6,7},{7,6},{8,9},{9,8},{10,11... | collective-permute-start | bytes 1327112 | tf_op jit(solution)/shard_map/ppermute | solution.py:320
  90.7 4.7 %collective-permute-start.19 = (f32[32,128]{1,0:T(8,128)S(1)}, f32[32,128]{1,0:T(8,128)S(1)}, u32[]{:S(2)}, u32[]{:S(2)}) collective-permute-start(f32[32,128]{1,0:T(8,128)S(1)} %add.52), channel_id=1, source_target_pairs={{0,2},{1,3},{2,0},{3,1},{4,6},{5,7},{6,4},{7,5},{8,10},{9,11},{10,... | collective-permute-start | bytes 49160 | tf_op jit(solution)/shard_map/ppermute | solution.py:323
  95.3 4.7 %collective-permute-start.20 = (f32[32,128]{1,0:T(8,128)S(1)}, f32[32,128]{1,0:T(8,128)S(1)}, u32[]{:S(2)}, u32[]{:S(2)}) collective-permute-start(f32[32,128]{1,0:T(8,128)S(1)} %add.53), channel_id=1, source_target_pairs={{0,4},{1,5},{2,6},{3,7},{4,0},{5,1},{6,2},{7,3},{8,12},{9,13},{10,... | collective-permute-start | bytes 49160 | tf_op jit(solution)/shard_map/ppermute | solution.py:323
  100.1 11.1 %collective-permute-start.21 = (f32[32,128]{1,0:T(8,128)S(1)}, f32[32,128]{1,0:T(8,128)S(1)}, u32[]{:S(2)}, u32[]{:S(2)}) collective-permute-start(f32[32,128]{1,0:T(8,128)S(1)} %add.54), channel_id=1, source_target_pairs={{0,8},{1,9},{2,10},{3,11},{4,12},{5,13},{6,14},{7,15},{8,0},{9,1},... | collective-permute-start | bytes 49160 | tf_op jit(solution)/shard_map/ppermute | solution.py:323
  111.2 4.1 %collective-permute-start.22 = (f32[32,128]{1,0:T(8,128)S(1)}, f32[32,128]{1,0:T(8,128)S(1)}, u32[]{:S(2)}, u32[]{:S(2)}) collective-permute-start(f32[32,128]{1,0:T(8,128)S(1)} %add.55.mine), channel_id=1, source_target_pairs={{0,1},{1,0},{2,3},{3,2},{4,5},{5,4},{6,7},{7,6},{8,9},{9,8},{10,11... | collective-permute-start | bytes 49160 | tf_op jit(solution)/shard_map/ppermute | solution.py:323
  (2 other events, 4.7 us)

commit v4 on v3

--- a/solution.py
+++ b/solution.py
@@ -11,7 +11,7 @@
 EPS = 1e-06
 LOG2_E = 1.4426950408889634
 LN_2 = 0.6931471805599453
-ROUNDS = ((16,), (32,), (64,), (128,), (2,), (4,), (8,), 1)
+ROUNDS = ((16,), (32,), (64,), (128,), (2,), (4,), (14,), 1)
 VMEM_LIMIT = 24 * 1024 * 1024
 SMEM = pl.BlockSpec(memory_space=pltpu.SMEM)
 VMEM = pl.BlockSpec(memory_space=pltpu.VMEM)

time: 119 us -> 118 us (level)
  starting transfers between devices: 36 us -> 34.7 us
    ppermute x8, starting transfers between devices: 14.1 us -> 12.8 us  [exchanged(): return lax.ppermute(value, 'dp', [(d, d ^ distance) for d in range(count)])]
where the time goes in v4:
time: 118 us; the launch traced here: 116 us
  Pallas kernels  43.7 us (37%)
  starting transfers between devices  34.7 us (29%)
  waiting for transfers between devices  34.5 us (29%)
  between operations  2.5 us (2%)
    pallas_call x14, Pallas kernels, stage(): pl.pallas_call(functools.partial(stage_kernel, plan), out_shape=out_shape...  34.8 us
    ppermute x3, starting transfers between devices, up(): return lax.ppermute(value, 'dp', up_down)  15 us
    ppermute x8, waiting for transfers between devices, exchanged(): return lax.ppermute(value, 'dp', [(d, d ^ distance) for d in range(count)])  13.8 us
    ppermute x8, starting transfers between devices, exchanged(): return lax.ppermute(value, 'dp', [(d, d ^ distance) for d in range(count)])  12.8 us
    ppermute x3, waiting for transfers between devices, up(): return lax.ppermute(value, 'dp', up_down)  10.5 us
    ppermute x3, waiting for transfers between devices, down(): return lax.ppermute(value, 'dp', down_up)  10.2 us
    ppermute x1, starting transfers between devices, per_device(): last, from_p3 = (lax.ppermute(p3, 'dp', cross), swap(p3))  6.09 us
    pallas_call x3, Pallas kernels, middle(): pl.pallas_call(functools.partial(middle_kernel, plan), out_shape=jax.Shap...  5.74 us
  transfers between devices with their start and end apart: 23, of which 8 were waited for; matrix products, arithmetic and copies ran while one was open for 0% of the time, Pallas kernels for 35%

profile of v4, /device:TPU:16, one launch (start us, length us, event | category | flops | bytes accessed | tf_op | source)
XLA Modules:
  0.0 116.1 jit_solution(12759160578689786527)
XLA Ops:
  2.5 5.8 %collective-permute-start = (bf16[384,1152]{1,0:T(8,128)(2,1)S(1)}, bf16[384,1152]{1,0:T(8,128)(2,1)S(1)}, u32[]{:S(2)}, u32[]{:S(2)}) collective-permute-start(bf16[384,1152]{1,0:T(8,128)(2,1)S(1)} %get-tuple-element.66.refs_1_.refs_2_), channel_id=1, source_target_pairs={{0,254},{1,3},{2,0},{3,5},{4,2},{5,7},{6,4},{7,9},{8,6},{9,11},{10... | collective-permute-start | bytes 2654216 | tf_op jit(solution)/shard_map/ppermute | solution.py:314
  9.7 2.2 %shard_map.68 = (f32[384,1152]{1,0:T(8,128)S(1)}, f32[32,128]{1,0:T(8,128)S(1)}) custom-call(f32[4]{0:T(128)S(1)} %pad_maximum_fusion.refs_0_.scalars, bf16[384,1152]{1,0:T(8,128)(2,1)S(1)} %get-tuple-element.66.refs_1_.refs_2_, bf16[384,1152]{1,0:T(8,128)(2,1)S(1)} %get-tuple-element.73.refs_2_.refs_1_), custom_call_target="tpu_custom_call" | custom-call | flops 1 | bytes 1 | tf_op jit(solution)/shard_map/pallas_call | solution.py:267
  12.0 2.6 %shard_map.69 = (f32[384,1152]{1,0:T(8,128)S(1)}, f32[32,128]{1,0:T(8,128)S(1)}) custom-call(f32[4]{0:T(128)S(1)} %pad_maximum_fusion.refs_0_.scalars, bf16[384,1152]{1,0:T(8,128)(2,1)S(1)} %get-tuple-element.73.refs_2_.refs_1_, bf16[384,1152]{1,0:T(8,128)(2,1)S(1)} %get-tuple-element.66.refs_1_.refs_2_, bf16[384,1152]{1,0:T(8,128)(2,1)S(1)} %collective-permute-done.1.refs_3_), custom_call_target="tpu_custom_call" | custom-call | flops 1 | bytes 1 | tf_op jit(solution)/shard_map/pallas_call | solution.py:267
  14.7 7.8 %collective-permute-done.refs_2_.refs_1_ = bf16[384,1152]{1,0:T(8,128)(2,1)S(1)} collective-permute-done((bf16[384,1152]{1,0:T(8,128)(2,1)S(1)}, bf16[384,1152]{1,0:T(8,128)(2,1)S(1)}, u32[]{:S(2)}, u32[]{:S(2)}) %collective-permute-start) | collective-permute-done | bytes 884768 | tf_op jit(solution)/shard_map/ppermute | solution.py:314
  22.5 4.6 %collective-permute-start.2 = (bf16[384,1152]{1,0:T(8,128)(2,1)S(1)}, bf16[384,1152]{1,0:T(8,128)(2,1)S(1)}, u32[]{:S(2)}, u32[]{:S(2)}) collective-permute-start(bf16[384,1152]{1,0:T(8,128)(2,1)S(1)} %collective-permute-done.refs_2_.refs_1_), channel_id=1, source_target_pairs={{0,254},{1,3},{2,0},{3,5},{4,2},{5,7},{6,4},{7,9},{8,6},{9,11},{10... | collective-permute-start | bytes 2654216 | tf_op jit(solution)/shard_map/ppermute | solution.py:314
  27.1 2.2 %shard_map.70 = (f32[384,1152]{1,0:T(8,128)S(1)}, f32[32,128]{1,0:T(8,128)S(1)}) custom-call(f32[4]{0:T(128)S(1)} %pad_maximum_fusion.refs_0_.scalars, bf16[384,1152]{1,0:T(8,128)(2,1)S(1)} %get-tuple-element.73.refs_2_.refs_1_, bf16[384,1152]{1,0:T(8,128)(2,1)S(1)} %collective-permute-done.refs_2_.refs_1_, ...), custom_call_target="tpu_custom_call", output_to_operand_aliasing={{0}: (3, {})} | custom-call | flops 1 | bytes 1 | tf_op jit(solution)/shard_map/pallas_call | solution.py:267
  29.3 6.8 %collective-permute-done.4.refs_2_ = bf16[384,1152]{1,0:T(8,128)(2,1)S(1)} collective-permute-done((bf16[384,1152]{1,0:T(8,128)(2,1)S(1)}, bf16[384,1152]{1,0:T(8,128)(2,1)S(1)}, u32[]{:S(2)}, u32[]{:S(2)}) %collective-permute-start.4) | collective-permute-done | bytes 884768 | tf_op jit(solution)/shard_map/ppermute | solution.py:317
  37.6 2.0 %shard_map.71.refs_3_ = f32[384,1152]{1,0:T(8,128)S(1)} custom-call(f32[4]{0:T(128)S(1)} %pad_maximum_fusion.refs_0_.scalars, bf16[384,1152]{1,0:T(8,128)(2,1)S(1)} %get-tuple-element.66.refs_1_.refs_2_, bf16[384,1152]{1,0:T(8,128)(2,1)S(1)} %collective-permute-done.4.refs_2_, f32[384,1152]{1,0:T(8,128)S(1)} %get-tuple-element.77.refs_3_), custom_call_target="tpu_custom_call", output_to_operand_aliasing={{}: (3, {})} | custom-call | flops 1 | bytes 1 | tf_op jit(solution)/shard_map/pallas_call | solution.py:267
  39.6 2.7 %collective-permute-done.2.refs_1_.refs_3_.refs_2_ = bf16[384,1152]{1,0:T(8,128)(2,1)S(1)} collective-permute-done((bf16[384,1152]{1,0:T(8,128)(2,1)S(1)}, bf16[384,1152]{1,0:T(8,128)(2,1)S(1)}, u32[]{:S(2)}, u32[]{:S(2)}) %collective-permute-start.2) | collective-permute-done | bytes 884768 | tf_op jit(solution)/shard_map/ppermute | solution.py:314
  42.3 4.6 %collective-permute-start.5 = (bf16[384,1152]{1,0:T(8,128)(2,1)S(1)}, bf16[384,1152]{1,0:T(8,128)(2,1)S(1)}, u32[]{:S(2)}, u32[]{:S(2)}) collective-permute-start(bf16[384,1152]{1,0:T(8,128)(2,1)S(1)} %collective-permute-done.2.refs_1_.refs_3_.refs_2_), channel_id=1, source_target_pairs={{0,254},{1,3},{2,0},{3,5},{4,2},{5,7},{6,4},{7,9},{8,6},{9,11},{10... | collective-permute-start | bytes 2654216 | tf_op jit(solution)/shard_map/ppermute | solution.py:314
  48.4 2.2 %shard_map.73 = (f32[384,1152]{1,0:T(8,128)S(1)}, f32[32,128]{1,0:T(8,128)S(1)}) custom-call(f32[4]{0:T(128)S(1)} %pad_maximum_fusion.refs_0_.scalars, bf16[384,1152]{1,0:T(8,128)(2,1)S(1)} %get-tuple-element.66.refs_1_.refs_2_, bf16[384,1152]{1,0:T(8,128)(2,1)S(1)} %collective-permute-done.3.refs_2_.refs_5_, ...), custom_call_target="tpu_custom_call", output_to_operand_aliasing={{0}: (3, {})} | custom-call | flops 1 | bytes 1 | tf_op jit(solution)/shard_map/pallas_call | solution.py:267
  50.6 3.4 %collective-permute-done.7.refs_4_.refs_2_ = bf16[384,1152]{1,0:T(8,128)(2,1)S(1)} collective-permute-done((bf16[384,1152]{1,0:T(8,128)(2,1)S(1)}, bf16[384,1152]{1,0:T(8,128)(2,1)S(1)}, u32[]{:S(2)}, u32[]{:S(2)}) %collective-permute-start.7) | collective-permute-done | bytes 884768 | tf_op jit(solution)/shard_map/ppermute | solution.py:317
  54.1 2.2 %shard_map.75 = (f32[384,1152]{1,0:T(8,128)S(1)}, f32[32,128]{1,0:T(8,128)S(1)}) custom-call(f32[4]{0:T(128)S(1)} %pad_maximum_fusion.refs_0_.scalars, bf16[384,1152]{1,0:T(8,128)(2,1)S(1)} %get-tuple-element.73.refs_2_.refs_1_, bf16[384,1152]{1,0:T(8,128)(2,1)S(1)} %collective-permute-done.8.refs_2_.refs_6_, ...), custom_call_target="tpu_custom_call", output_to_operand_aliasing={{0}: (3, {})} | custom-call | flops 1 | bytes 1 | tf_op jit(solution)/shard_map/pallas_call | solution.py:267
  56.3 2.7 %shard_map.76 = f32[32,128]{1,0:T(8,128)S(1)} custom-call(f32[4]{0:T(128)S(1)} %pad_maximum_fusion.refs_0_.scalars, bf16[384,1152]{1,0:T(8,128)(2,1)S(1)} %collective-permute-done.refs_2_.refs_1_, bf16[384,1152]{1,0:T(8,128)(2,1)S(1)} %collective-permute-done.4.refs_2_, bf16[384,1152]{1,0:T(8,128)(2,1)S(1)} %collective-permute-done.2.refs_1_.refs_3_.refs_2_, ...), custom_call_target="tpu_custom_call" | custom-call | flops 1 | bytes 1 | tf_op jit(solution)/shard_map/pallas_call | solution.py:223
  60.7 2.0 %shard_map.77.refs_3_ = f32[384,1152]{1,0:T(8,128)S(1)} custom-call(f32[4]{0:T(128)S(1)} %pad_maximum_fusion.refs_0_.scalars, bf16[384,1152]{1,0:T(8,128)(2,1)S(1)} %get-tuple-element.66.refs_1_.refs_2_, bf16[384,1152]{1,0:T(8,128)(2,1)S(1)} %collective-permute-done.7.refs_4_.refs_2_, ...), custom_call_target="tpu_custom_call", output_to_operand_aliasing={{}: (3, {})} | custom-call | flops 1 | bytes 1 | tf_op jit(solution)/shard_map/pallas_call | solution.py:267
  62.8 6.9 %collective-permute-done.9 = f32[32,128]{1,0:T(8,128)S(1)} collective-permute-done((f32[32,128]{1,0:T(8,128)S(1)}, f32[32,128]{1,0:T(8,128)S(1)}, u32[]{:S(2)}, u32[]{:S(2)}) %collective-permute-start.9) | collective-permute-done | bytes 16416 | tf_op jit(solution)/shard_map/ppermute | solution.py:323
  69.6 5.0 %collective-permute-start.10 = (f32[32,128]{1,0:T(8,128)S(1)}, f32[32,128]{1,0:T(8,128)S(1)}, u32[]{:S(2)}, u32[]{:S(2)}) collective-permute-start(f32[32,128]{1,0:T(8,128)S(1)} %add.49), channel_id=1, source_target_pairs={{0,32},{1,33},{2,34},{3,35},{4,36},{5,37},{6,38},{7,39},{8,40},{9,... | collective-permute-start | bytes 49160 | tf_op jit(solution)/shard_map/ppermute | solution.py:323
  81.8 6.1 %collective-permute-start.11 = (bf16[384,1152]{1,0:T(8,128)(2,1)S(1)}, bf16[384,1152]{1,0:T(8,128)(2,1)S(1)}, u32[]{:S(2)}, u32[]{:S(2)}) collective-permute-start(bf16[384,1152]{1,0:T(8,128)(2,1)S(1)} %collective-permute-done.5.refs_2_), channel_id=1, source_target_pairs={{0,255},{1,2},{2,1},{3,4},{4,3},{5,6},{6,5},{7,8},{8,7},{9,10},{10... | collective-permute-start | bytes 2654216 | tf_op jit(solution)/shard_map/ppermute | solution.py:375
  87.9 2.0 %shard_map.80.refs_5_ = f32[384,1152]{1,0:T(8,128)S(1)} custom-call(f32[4]{0:T(128)S(1)} %pad_maximum_fusion.refs_0_.scalars, bf16[384,1152]{1,0:T(8,128)(2,1)S(1)} %get-tuple-element.73.refs_2_.refs_1_, bf16[384,1152]{1,0:T(8,128)(2,1)S(1)} %collective-permute-done.13.refs_2_, f32[384,1152]{1,0:T(8,128)S(1)} %shard_map.79.refs_3_), custom_call_target="tpu_custom_call", output_to_operand_aliasing={{}: (3, {})} | custom-call | flops 1 | bytes 1 | tf_op jit(solution)/shard_map/pallas_call | solution.py:267
  92.7 2.6 %collective-permute-done.19 = f32[32,128]{1,0:T(8,128)S(1)} collective-permute-done((f32[32,128]{1,0:T(8,128)S(1)}, f32[32,128]{1,0:T(8,128)S(1)}, u32[]{:S(2)}, u32[]{:S(2)}) %collective-permute-start.19) | collective-permute-done | bytes 16416 | tf_op jit(solution)/shard_map/ppermute | solution.py:323
  97.5 2.6 %collective-permute-done.20 = f32[32,128]{1,0:T(8,128)S(1)} collective-permute-done((f32[32,128]{1,0:T(8,128)S(1)}, f32[32,128]{1,0:T(8,128)S(1)}, u32[]{:S(2)}, u32[]{:S(2)}) %collective-permute-start.20) | collective-permute-done | bytes 16416 | tf_op jit(solution)/shard_map/ppermute | solution.py:323
  100.1 4.2 %collective-permute-start.21 = (f32[32,128]{1,0:T(8,128)S(1)}, f32[32,128]{1,0:T(8,128)S(1)}, u32[]{:S(2)}, u32[]{:S(2)}) collective-permute-start(f32[32,128]{1,0:T(8,128)S(1)} %add.54), channel_id=1, source_target_pairs={{0,14},{1,15},{2,12},{3,13},{4,10},{5,11},{6,8},{7,9},{8,6},{9,7},... | collective-permute-start | bytes 49160 | tf_op jit(solution)/shard_map/ppermute | solution.py:323
  104.3 5.2 %shard_map.83 = (f32[384,1152]{1,0:T(8,128)}, f32[384,1152]{1,0:T(8,128)}) custom-call(f32[4]{0:T(128)S(1)} %pad_maximum_fusion.refs_0_.scalars, bf16[384,1152]{1,0:T(8,128)(2,1)S(1)} %get-tuple-element.73.refs_2_.refs_1_, bf16[384,1152]{1,0:T(8,128)(2,1)S(1)} %collective-permute-done.5.refs_2_, bf16[192,1152]{1,0:T(8,128)(2,1)S(1)} %collective-permute-done.16.refs_3_, ...), custom_call_target="tpu_custom_call" | custom-call | flops 1 | bytes 1 | tf_op jit(solution)/shard_map/pallas_call | solution.py:267
  110.0 3.9 %shard_map.84 = (f32[384,1152]{1,0:T(8,128)}, f32[384,1152]{1,0:T(8,128)}) custom-call(f32[4]{0:T(128)S(1)} %pad_maximum_fusion.refs_0_.scalars, bf16[384,1152]{1,0:T(8,128)(2,1)S(1)} %get-tuple-element.66.refs_1_.refs_2_, bf16[384,1152]{1,0:T(8,128)(2,1)S(1)} %collective-permute-done.11.refs_2_, ...), custom_call_target="tpu_custom_call", output_to_operand_aliasing={{0}: (6, {}), {1}: (7, {})} | custom-call | flops 1 | bytes 1 | tf_op jit(solution)/shard_map/pallas_call | solution.py:267
  (57 shorter events, 21.1 us)
Async XLA Ops:
  2.4 9.6 %collective-permute-start.1 = (bf16[384,1152]{1,0:T(8,128)(2,1)S(1)}, bf16[384,1152]{1,0:T(8,128)(2,1)S(1)}, u32[]{:S(2)}, u32[]{:S(2)}) collective-permute-start(bf16[384,1152]{1,0:T(8,128)(2,1)S(1)} %get-tuple-element.73.refs_2_.refs_1_), channel_id=1, source_target_pairs={{0,1},{1,0},{2,3},{3,2},{4,5},{5,4},{6,7},{7,6},{8,9},{9,8},{10,11... | collective-permute-start | bytes 2654216 | tf_op jit(solution)/shard_map/ppermute | solution.py:320
  2.5 20.0 %collective-permute-start = (bf16[384,1152]{1,0:T(8,128)(2,1)S(1)}, bf16[384,1152]{1,0:T(8,128)(2,1)S(1)}, u32[]{:S(2)}, u32[]{:S(2)}) collective-permute-start(bf16[384,1152]{1,0:T(8,128)(2,1)S(1)} %get-tuple-element.66.refs_1_.refs_2_), channel_id=1, source_target_pairs={{0,254},{1,3},{2,0},{3,5},{4,2},{5,7},{6,4},{7,9},{8,6},{9,11},{10... | collective-permute-start | bytes 2654216 | tf_op jit(solution)/shard_map/ppermute | solution.py:314
  9.7 100.3 %copy-start = (f32[4]{0:T(128)}, f32[4]{0:T(128)S(1)}, u32[]{:S(2)}) copy-start(f32[4]{0:T(128)S(1)} %pad_maximum_fusion.refs_0_.scalars) | copy-start | bytes 52
  14.6 21.4 %collective-permute-start.4 = (bf16[384,1152]{1,0:T(8,128)(2,1)S(1)}, bf16[384,1152]{1,0:T(8,128)(2,1)S(1)}, u32[]{:S(2)}, u32[]{:S(2)}) collective-permute-start(bf16[384,1152]{1,0:T(8,128)(2,1)S(1)} %get-tuple-element.73.refs_2_.refs_1_), channel_id=1, source_target_pairs={{0,2},{1,255},{2,4},{3,1},{4,6},{5,3},{6,8},{7,5},{8,10},{9,7},{10... | collective-permute-start | bytes 2654216 | tf_op jit(solution)/shard_map/ppermute | solution.py:317
  22.5 19.8 %collective-permute-start.2 = (bf16[384,1152]{1,0:T(8,128)(2,1)S(1)}, bf16[384,1152]{1,0:T(8,128)(2,1)S(1)}, u32[]{:S(2)}, u32[]{:S(2)}) collective-permute-start(bf16[384,1152]{1,0:T(8,128)(2,1)S(1)} %collective-permute-done.refs_2_.refs_1_), channel_id=1, source_target_pairs={{0,254},{1,3},{2,0},{3,5},{4,2},{5,7},{6,4},{7,9},{8,6},{9,11},{10... | collective-permute-start | bytes 2654216 | tf_op jit(solution)/shard_map/ppermute | solution.py:314
  27.1 15.2 %collective-permute-start.3 = (bf16[384,1152]{1,0:T(8,128)(2,1)S(1)}, bf16[384,1152]{1,0:T(8,128)(2,1)S(1)}, u32[]{:S(2)}, u32[]{:S(2)}) collective-permute-start(bf16[384,1152]{1,0:T(8,128)(2,1)S(1)} %collective-permute-done.refs_2_.refs_1_), channel_id=1, source_target_pairs={{0,1},{1,0},{2,3},{3,2},{4,5},{5,4},{6,7},{7,6},{8,9},{9,8},{10,11... | collective-permute-start | bytes 2654216 | tf_op jit(solution)/shard_map/ppermute | solution.py:320
  36.0 18.0 %collective-permute-start.7 = (bf16[384,1152]{1,0:T(8,128)(2,1)S(1)}, bf16[384,1152]{1,0:T(8,128)(2,1)S(1)}, u32[]{:S(2)}, u32[]{:S(2)}) collective-permute-start(bf16[384,1152]{1,0:T(8,128)(2,1)S(1)} %collective-permute-done.4.refs_2_), channel_id=1, source_target_pairs={{0,2},{1,255},{2,4},{3,1},{4,6},{5,3},{6,8},{7,5},{8,10},{9,7},{10... | collective-permute-start | bytes 2654216 | tf_op jit(solution)/shard_map/ppermute | solution.py:317
  36.0 18.0 %collective-permute-start.8 = (bf16[384,1152]{1,0:T(8,128)(2,1)S(1)}, bf16[384,1152]{1,0:T(8,128)(2,1)S(1)}, u32[]{:S(2)}, u32[]{:S(2)}) collective-permute-start(bf16[384,1152]{1,0:T(8,128)(2,1)S(1)} %collective-permute-done.4.refs_2_), channel_id=1, source_target_pairs={{0,1},{1,0},{2,3},{3,2},{4,5},{5,4},{6,7},{7,6},{8,9},{9,8},{10,11... | collective-permute-start | bytes 2654216 | tf_op jit(solution)/shard_map/ppermute | solution.py:320
  42.3 14.0 %collective-permute-start.6 = (bf16[384,1152]{1,0:T(8,128)(2,1)S(1)}, bf16[384,1152]{1,0:T(8,128)(2,1)S(1)}, u32[]{:S(2)}, u32[]{:S(2)}) collective-permute-start(bf16[384,1152]{1,0:T(8,128)(2,1)S(1)} %collective-permute-done.2.refs_1_.refs_3_.refs_2_), channel_id=1, source_target_pairs={{0,1},{1,0},{2,3},{3,2},{4,5},{5,4},{6,7},{7,6},{8,9},{9,8},{10,11... | collective-permute-start | bytes 2654216 | tf_op jit(solution)/shard_map/ppermute | solution.py:320
  42.3 34.4 %collective-permute-start.5 = (bf16[384,1152]{1,0:T(8,128)(2,1)S(1)}, bf16[384,1152]{1,0:T(8,128)(2,1)S(1)}, u32[]{:S(2)}, u32[]{:S(2)}) collective-permute-start(bf16[384,1152]{1,0:T(8,128)(2,1)S(1)} %collective-permute-done.2.refs_1_.refs_3_.refs_2_), channel_id=1, source_target_pairs={{0,254},{1,3},{2,0},{3,5},{4,2},{5,7},{6,4},{7,9},{8,6},{9,11},{10... | collective-permute-start | bytes 2654216 | tf_op jit(solution)/shard_map/ppermute | solution.py:314
  54.1 26.5 %collective-permute-start.13 = (bf16[384,1152]{1,0:T(8,128)(2,1)S(1)}, bf16[384,1152]{1,0:T(8,128)(2,1)S(1)}, u32[]{:S(2)}, u32[]{:S(2)}) collective-permute-start(bf16[384,1152]{1,0:T(8,128)(2,1)S(1)} %collective-permute-done.7.refs_4_.refs_2_), channel_id=1, source_target_pairs={{0,1},{1,0},{2,3},{3,2},{4,5},{5,4},{6,7},{7,6},{8,9},{9,8},{10,11... | collective-permute-start | bytes 2654216 | tf_op jit(solution)/shard_map/ppermute | solution.py:320
  54.1 35.9 %collective-permute-start.12 = (bf16[384,1152]{1,0:T(8,128)(2,1)S(1)}, bf16[384,1152]{1,0:T(8,128)(2,1)S(1)}, u32[]{:S(2)}, u32[]{:S(2)}) collective-permute-start(bf16[384,1152]{1,0:T(8,128)(2,1)S(1)} %collective-permute-done.7.refs_4_.refs_2_), channel_id=1, source_target_pairs={{0,2},{1,255},{2,4},{3,1},{4,6},{5,3},{6,8},{7,5},{8,10},{9,7},{10... | collective-permute-start | bytes 2654216 | tf_op jit(solution)/shard_map/ppermute | solution.py:317
  59.1 10.6 %collective-permute-start.9 = (f32[32,128]{1,0:T(8,128)S(1)}, f32[32,128]{1,0:T(8,128)S(1)}, u32[]{:S(2)}, u32[]{:S(2)}) collective-permute-start(f32[32,128]{1,0:T(8,128)S(1)} %add_add_fusion), channel_id=1, source_target_pairs={{0,16},{1,17},{2,18},{3,19},{4,20},{5,21},{6,22},{7,23},{8,24},{9,... | collective-permute-start | bytes 49160 | tf_op jit(solution)/shard_map/ppermute | solution.py:323
  69.6 7.0 %collective-permute-start.10 = (f32[32,128]{1,0:T(8,128)S(1)}, f32[32,128]{1,0:T(8,128)S(1)}, u32[]{:S(2)}, u32[]{:S(2)}) collective-permute-start(f32[32,128]{1,0:T(8,128)S(1)} %add.49), channel_id=1, source_target_pairs={{0,32},{1,33},{2,34},{3,35},{4,36},{5,37},{6,38},{7,39},{8,40},{9,... | collective-permute-start | bytes 49160 | tf_op jit(solution)/shard_map/ppermute | solution.py:323
  76.7 3.8 %collective-permute-start.14 = (f32[32,128]{1,0:T(8,128)S(1)}, f32[32,128]{1,0:T(8,128)S(1)}, u32[]{:S(2)}, u32[]{:S(2)}) collective-permute-start(f32[32,128]{1,0:T(8,128)S(1)} %add.50), channel_id=1, source_target_pairs={{0,64},{1,65},{2,66},{3,67},{4,68},{5,69},{6,70},{7,71},{8,72},{9,... | collective-permute-start | bytes 49160 | tf_op jit(solution)/shard_map/ppermute | solution.py:323
  80.5 9.4 %collective-permute-start.15 = (f32[32,128]{1,0:T(8,128)S(1)}, f32[32,128]{1,0:T(8,128)S(1)}, u32[]{:S(2)}, u32[]{:S(2)}) collective-permute-start(f32[32,128]{1,0:T(8,128)S(1)} %add.51), channel_id=1, source_target_pairs={{0,128},{1,129},{2,130},{3,131},{4,132},{5,133},{6,134},{7,135},{8... | collective-permute-start | bytes 49160 | tf_op jit(solution)/shard_map/ppermute | solution.py:323
  81.8 13.5 %collective-permute-start.18 = (bf16[384,1152]{1,0:T(8,128)(2,1)S(1)}, bf16[384,1152]{1,0:T(8,128)(2,1)S(1)}, u32[]{:S(2)}, u32[]{:S(2)}) collective-permute-start(bf16[384,1152]{1,0:T(8,128)(2,1)S(1)} %collective-permute-done.5.refs_2_), channel_id=1, source_target_pairs={{0,1},{1,0},{2,3},{3,2},{4,5},{5,4},{6,7},{7,6},{8,9},{9,8},{10,11... | collective-permute-start | bytes 2654216 | tf_op jit(solution)/shard_map/ppermute | solution.py:320
  81.8 27.8 %collective-permute-start.11 = (bf16[384,1152]{1,0:T(8,128)(2,1)S(1)}, bf16[384,1152]{1,0:T(8,128)(2,1)S(1)}, u32[]{:S(2)}, u32[]{:S(2)}) collective-permute-start(bf16[384,1152]{1,0:T(8,128)(2,1)S(1)} %collective-permute-done.5.refs_2_), channel_id=1, source_target_pairs={{0,255},{1,2},{2,1},{3,4},{4,3},{5,6},{6,5},{7,8},{8,7},{9,10},{10... | collective-permute-start | bytes 2654216 | tf_op jit(solution)/shard_map/ppermute | solution.py:375
  90.1 10.0 %collective-permute-start.16 = (bf16[192,1152]{1,0:T(8,128)(2,1)S(1)}, bf16[192,1152]{1,0:T(8,128)(2,1)S(1)}, u32[]{:S(2)}, u32[]{:S(2)}) collective-permute-start(bf16[192,1152]{1,0:T(8,128)(2,1)S(1)} %get-tuple-element.130), channel_id=1, source_target_pairs={{0,1},{1,0},{2,3},{3,2},{4,5},{5,4},{6,7},{7,6},{8,9},{9,8},{10,11... | collective-permute-start | bytes 1327112 | tf_op jit(solution)/shard_map/ppermute | solution.py:320
  90.2 9.9 %collective-permute-start.17 = (bf16[192,1152]{1,0:T(8,128)(2,1)S(1)}, bf16[192,1152]{1,0:T(8,128)(2,1)S(1)}, u32[]{:S(2)}, u32[]{:S(2)}) collective-permute-start(bf16[192,1152]{1,0:T(8,128)(2,1)S(1)} %get-tuple-element.129), channel_id=1, source_target_pairs={{0,1},{1,0},{2,3},{3,2},{4,5},{5,4},{6,7},{7,6},{8,9},{9,8},{10,11... | collective-permute-start | bytes 1327112 | tf_op jit(solution)/shard_map/ppermute | solution.py:320
  90.7 4.7 %collective-permute-start.19 = (f32[32,128]{1,0:T(8,128)S(1)}, f32[32,128]{1,0:T(8,128)S(1)}, u32[]{:S(2)}, u32[]{:S(2)}) collective-permute-start(f32[32,128]{1,0:T(8,128)S(1)} %add.52), channel_id=1, source_target_pairs={{0,2},{1,3},{2,0},{3,1},{4,6},{5,7},{6,4},{7,5},{8,10},{9,11},{10,... | collective-permute-start | bytes 49160 | tf_op jit(solution)/shard_map/ppermute | solution.py:323
  95.3 4.7 %collective-permute-start.20 = (f32[32,128]{1,0:T(8,128)S(1)}, f32[32,128]{1,0:T(8,128)S(1)}, u32[]{:S(2)}, u32[]{:S(2)}) collective-permute-start(f32[32,128]{1,0:T(8,128)S(1)} %add.53), channel_id=1, source_target_pairs={{0,4},{1,5},{2,6},{3,7},{4,0},{5,1},{6,2},{7,3},{8,12},{9,13},{10,... | collective-permute-start | bytes 49160 | tf_op jit(solution)/shard_map/ppermute | solution.py:323
  100.1 9.5 %collective-permute-start.21 = (f32[32,128]{1,0:T(8,128)S(1)}, f32[32,128]{1,0:T(8,128)S(1)}, u32[]{:S(2)}, u32[]{:S(2)}) collective-permute-start(f32[32,128]{1,0:T(8,128)S(1)} %add.54), channel_id=1, source_target_pairs={{0,14},{1,15},{2,12},{3,13},{4,10},{5,11},{6,8},{7,9},{8,6},{9,7},... | collective-permute-start | bytes 49160 | tf_op jit(solution)/shard_map/ppermute | solution.py:323
  109.6 4.4 %collective-permute-start.22 = (f32[32,128]{1,0:T(8,128)S(1)}, f32[32,128]{1,0:T(8,128)S(1)}, u32[]{:S(2)}, u32[]{:S(2)}) collective-permute-start(f32[32,128]{1,0:T(8,128)S(1)} %add.55.mine), channel_id=1, source_target_pairs={{0,1},{1,0},{2,3},{3,2},{4,5},{5,4},{6,7},{7,6},{8,9},{9,8},{10,11... | collective-permute-start | bytes 49160 | tf_op jit(solution)/shard_map/ppermute | solution.py:323
  (2 other events, 5.0 us)
